TPU v7x, 32 devices: a whole 2x2x4 slice. The times are simulated.
32 devices in a mesh: leaf: 32 (over z, y, x, core).
Axes of the slice: x: 2, y: 2, z: 4, core: 2. Of those that a mesh axis runs over, the one named last changes fastest.
Arguments:
- points: float32 [16, 65536], P(None, 'leaf'), may hold values from -6 to 6
- order: int32 [65536], P('leaf'), may hold values from 0 to 65535, as said below
- bases: float32 [256, 256, 64], P('leaf'), may hold values from -0.375 to 0.375
- lift: float32 [256, 64, 64], P('leaf'), may hold values from -0.25 to 0.25
- near_ids: int32 [256, 3], P('leaf'), may hold values from 0 to 255, as said below
- near_blocks: float32 [256, 3, 256, 256], P('leaf'), may hold values from -0.21875 to 0.21875
- far_ids: int32 [256, 8], P('leaf'), may hold values from 0 to 255, as said below
- far_count: int32 [256], P('leaf'), may hold values from 1 to 8
- far_blocks: float32 [256, 8, 64, 64], P('leaf'), may hold values from -0.25 to 0.25
- transfer: float32 [4, 2, 64, 64], replicated, may hold values from -0.5 to 0.5
- couple: float32 [4, 4, 64, 64], replicated, may hold values from -0.375 to 0.375
- links: int32 [32, 4, 4], P('leaf'), may hold values from 0 to 1, as said below
- top_couple: float32 [64, 64], replicated, may hold values from -0.75 to 0.75
Outputs:
- product: float32 [16, 65536], P(None, 'leaf')
Inputs may be any that keep to these rules, and one draw needn't show every extreme that they name: `order`: each subtree's 2048 entries are a permutation of that subtree's positions. `near_ids`: the first entry of a leaf is the leaf itself; the others lie at most one leaf away. `far_ids`: a coupled leaf lies in a subtree at most 4 subtrees away from the leaf's own; slots at or beyond far_count are padding. links[d, l, k] is the same for all d in one aligned block of 2^l subtrees.
All inputs are finite; a program needn't handle non-finite values.
Results may differ from a plain program's by a relative error of at most 0.0001.
Values sent between devices are 32-bit elements; how exact they have to be, the bound alone decides.
No kernel may reach another device: no remote copies, remote signals or barrier semaphores. Data moves between devices by JAX's collectives and lax.ppermute only.
A program may use at most 64 MiB of HBM per device.

v0:
```python
import functools

import jax
import jax.numpy as jnp
from jax import lax
from jax.experimental import pallas as pl
from jax.experimental.pallas import tpu as pltpu
from jax.sharding import PartitionSpec as P

REACH = 4
DEPTH = 4
OFFSETS = (-3, -2, 2, 3)
GROUP = 2 * REACH
LANES = 128
TILE = 8
NODES = GROUP - 1
VMEM_LIMIT = 64 * 1024 * 1024

NN = (((1,), (0,)), ((), ()))
NT = (((1,), (1,)), ((), ()))

VMEM = pl.BlockSpec(memory_space=pltpu.VMEM)
SMEM = pl.BlockSpec(memory_space=pltpu.SMEM)
HBM = pl.BlockSpec(memory_space=pltpu.HBM)
PARAMS = pltpu.CompilerParams(vmem_limit_bytes=VMEM_LIMIT)
F32 = jnp.float32
BF16 = jnp.bfloat16


def halves(x):
    high = x.astype(BF16)
    low = (x - high.astype(F32)).astype(BF16)
    return high, low


def dot_halves(a, b_high, b_low, dims):
    a_high, a_low = halves(a)
    rows = a.shape[0]
    both = lax.dot_general(
        jnp.concatenate([a_high, a_low], axis=0), b_high, dims, preferred_element_type=F32
    )
    cross = lax.dot_general(a_high, b_low, dims, preferred_element_type=F32)
    return both[:rows] + (both[rows:] + cross)


def pair_dot(a, b, w_high, w_low):
    a_high, a_low = halves(a)
    b_high, b_low = halves(b)
    rows = a.shape[0]
    both = lax.dot_general(
        jnp.concatenate([a_high, b_high, a_low, b_low], axis=0),
        w_high,
        NN,
        preferred_element_type=F32,
    )
    cross = lax.dot_general(
        jnp.concatenate([a_high, b_high], axis=0), w_low, NN, preferred_element_type=F32
    )
    total = both[: 2 * rows] + (both[2 * rows :] + cross)
    return total[:rows], total[rows:]


def dot3(a, b, dims):
    return dot_halves(a, *halves(b), dims)


def fold(x):
    return jnp.concatenate([x[:TILE], x[TILE:]], axis=1)


def beside(p, q):
    rank = p.shape[1] // 2
    left = lax.broadcasted_iota(jnp.int32, p.shape, 1) < rank
    return jnp.concatenate(
        [
            jnp.where(left, p, pltpu.roll(q, rank, 1)),
            jnp.where(left, pltpu.roll(p, rank, 1), q),
        ],
        axis=0,
    )


def row_of(tiles):
    return jnp.concatenate([beside(*tiles[k : k + 2]) for k in range(0, len(tiles), 2)], axis=1)


def lane_gather(x, high, low):
    rows, columns = x.shape
    high = jnp.broadcast_to(high, (rows, LANES))
    low = jnp.broadcast_to(low, (rows, LANES))
    result = jnp.zeros((rows, LANES), x.dtype)
    for source in range(columns // LANES):
        tile = x[:, source * LANES : (source + 1) * LANES]
        moved = jnp.take_along_axis(tile, low, axis=1, mode="promise_in_bounds")
        result = jnp.where(high == source, moved, result)
    return result


def fetch(pairs, sems):
    copies = [
        pltpu.make_async_copy(source, target, sems.at[index])
        for index, (source, target) in enumerate(pairs)
    ]
    for copy in copies:
        copy.start()
    return copies


def up_kernel(
    me_ref, points_hbm, order_hbm, bases_hbm, lift_hbm, out, x_out, points_v, order_v, bases_v, lift_v, sems
):
    copies = fetch(
        [(order_hbm, order_v), (points_hbm, points_v), (bases_hbm, bases_v), (lift_hbm, lift_v)], sems
    )
    me = me_ref[0]
    leaf_dev, rank, leaf_size = bases_v.shape
    vectors, points_dev = points_v.shape
    copies[0].wait()
    copies[1].wait()
    points = points_v[...]
    per_leaf = leaf_size // LANES
    for t in range(points_dev // LANES):
        spot = order_v[t : t + 1, :] - me * points_dev
        column = t % per_leaf * LANES
        x_out[t // per_leaf, :, column : column + LANES] = lane_gather(
            points, lax.shift_right_logical(spot, 7), spot & (LANES - 1)
        )
    copies[2].wait()
    coefs = [dot3(x_out[leaf], bases_v[leaf], NT) for leaf in range(leaf_dev)]
    tiles = [fold(coef) for coef in coefs]
    copies[3].wait()
    weights = lift_v[...].reshape(leaf_dev * rank, rank)
    tiles.append(fold(dot3(jnp.concatenate(coefs, axis=1), weights, NN)))
    for peer in range(GROUP):
        for index, tile in enumerate(tiles):
            out[peer, index * TILE : (index + 1) * TILE, :] = tile
    place = lax.rem(me, GROUP)
    start = len(tiles) * TILE
    for part in range(per_leaf):
        first = x_out[0, :, part * LANES : (part + 1) * LANES]
        last = x_out[leaf_dev - 1, :, part * LANES : (part + 1) * LANES]
        rows = slice(start + part * vectors, start + (part + 1) * vectors)
        for peer in range(GROUP):
            above = lax.rem(place + 1, GROUP) == peer
            out[peer, rows, :] = jnp.where(above, last, first)


def side_kernel(me_ref, *refs):
    inputs, outputs = refs[:11], refs[11:25]
    held, results = refs[25:36], refs[36:50]
    sems, block_sems, out_sems = refs[50:]
    ids_s, links_s, transfer_v, couple_v, x_v, top_v, lift_v, order_v, far_v, bases_v, blocks_v = held
    (
        up_high,
        up_low,
        path_high,
        path_low,
        inverse_out,
        leaf_high,
        leaf_low,
        lift_high,
        lift_low,
        bases_high,
        bases_low,
        edge_high,
        edge_low,
        near_out,
    ) = results
    leaf_dev, slots, leaf_size, _ = blocks_v.shape
    rank = top_v.shape[0]
    pairs = leaf_dev // 2
    me = me_ref[0]
    first = fetch(list(zip(inputs[:8], held[:8])), sems)

    def block(pair):
        two = pl.ds(2 * pair, 2)
        return fetch([(inputs[10].at[two], blocks_v.at[two])], block_sems.at[pl.ds(pair, 1)])

    blocks = block(0)
    second = fetch(list(zip(inputs[8:10], held[8:10])), sems.at[pl.ds(8, 2)])
    for pair in range(1, pairs):
        blocks += block(pair)
    writes = []

    def write(*indices):
        for index in indices:
            writes.extend(fetch([(results[index], outputs[index])], out_sems.at[pl.ds(index, 1)]))

    def couplings(level):
        weights = [
            links_s[level, column].astype(F32) * couple_v[level, column]
            for column in range(len(OFFSETS))
        ]
        return jnp.concatenate(weights, axis=1)

    def chain():
        bits = [lax.shift_right_logical(me, level) & 1 for level in range(DEPTH)]
        up = transfer_v[0].reshape(2 * rank, rank)
        path = transfer_v[0, bits[0]]
        parts = [couplings(0)]
        row = 0
        for level in range(1, DEPTH):
            rows = up.shape[0]
            up_high[row : row + rows], up_low[row : row + rows] = halves(up)
            row += rows
            if level < DEPTH - 1:
                up = jnp.concatenate(
                    [dot3(up, transfer_v[level, side], NN) for side in range(2)], axis=0
                )
            parts.append(dot3(path, couplings(level), NN))
            path = dot3(path, transfer_v[level, bits[level]], NN)
            if level < DEPTH - 1:
                yield
        write(0, 1)
        top = dot3(path, top_v[...], NN)
        yield
        parts = [x[:, k * rank : (k + 1) * rank] for x in parts for k in range(len(OFFSETS))]
        parts += [dot3(top, transfer_v[DEPTH - 1, side], NT) for side in range(2)]
        half = len(parts) // 2
        for index in range(half):
            span = slice(index * rank, (index + 1) * rank)
            both = jnp.concatenate([parts[index], parts[half + index]], axis=0).T
            path_high[span], path_low[span] = halves(both)
        write(2, 3)

    def inverse():
        points_dev = order_v.shape[1]
        tiles = points_dev // LANES
        spot = order_v[...] - me * points_dev
        times = lax.broadcasted_iota(jnp.int32, (1, points_dev), 1)
        shape = (tiles, points_dev)
        match = lax.broadcasted_iota(jnp.int32, shape, 0) == lax.shift_right_logical(spot, 7)
        digits = [
            jnp.where(match, jnp.broadcast_to(digit.astype(F32), shape), 0.0)
            for digit in (lax.shift_right_logical(times, 4), times & 15)
        ]
        shape = (LANES, points_dev)
        match = lax.broadcasted_iota(jnp.int32, shape, 0) == (spot & (LANES - 1))
        both = lax.dot_general(
            jnp.concatenate(digits, axis=0).astype(BF16),
            jnp.where(match, 1.0, 0.0).astype(BF16),
            NT,
            preferred_element_type=F32,
        )
        inverse_out[...] = (both[:tiles] * 16.0 + both[tiles:]).astype(jnp.int32)
        write(4)

    def transposes(pair):
        two = range(2 * pair, 2 * pair + 2)
        for slot in range(far_v.shape[1]):
            span = slice(slot * rank, (slot + 1) * rank)
            both = jnp.concatenate([far_v[leaf, slot] for leaf in two], axis=0).T
            leaf_high[pair, span], leaf_low[pair, span] = halves(both)
        both = jnp.concatenate([lift_v[leaf] for leaf in two], axis=0).T
        lift_high[pair], lift_low[pair] = halves(both)
        bases_high[pair], bases_low[pair] = halves(bases_v[pair])

    def near(leaf):
        total = jnp.zeros(near_out.shape[1:], F32)
        for slot in range(slots):
            local = ids_s[slot, leaf] - me * leaf_dev
            here = (local >= 0) & (local < leaf_dev)
            x_leaf = jnp.where(here, x_v[jnp.clip(local, 0, leaf_dev - 1)], 0.0)
            total = total + dot3(x_leaf, blocks_v[leaf, slot], NT)
        near_out[leaf] = total

    def edge(index, leaf, outside):
        total = jnp.zeros((leaf_size, leaf_size), F32)
        for slot in range(1, slots):
            remote = ids_s[slot, leaf] - me * leaf_dev == outside
            total = total + jnp.where(remote, blocks_v[leaf, slot], 0.0)
        edge_high[index], edge_low[index] = halves(total.T)

    for copy in first:
        copy.wait()
    links = chain()
    next(links)
    for pair in range(pairs):
        blocks[pair].wait()
        if pair == 0:
            for copy in second:
                copy.wait()
        near(2 * pair)
        near(2 * pair + 1)
        transposes(pair)
        next(links, None)
        if pair == 0:
            edge(0, 0, -1)
        if pair == 1:
            inverse()
        if pair == pairs - 1:
            edge(1, leaf_dev - 1, leaf_dev)
    for _ in links:
        pass
    write(*range(5, 14))
    for copy in writes:
        copy.wait()


def middle_kernel(
    leaf_dev,
    me_ref,
    group_hbm,
    up_high_hbm,
    up_low_hbm,
    half_out,
    nodes_out,
    far_out,
    roots_v,
    up_high,
    up_low,
    sems,
    half_sems,
):
    low = lax.rem(me_ref[0], GROUP) < REACH
    copies = fetch(
        [
            (group_hbm.at[:, pl.ds(leaf_dev * TILE, TILE), :], roots_v),
            (up_high_hbm, up_high),
            (up_low_hbm, up_low),
        ],
        sems,
    )
    rows = (leaf_dev + 1) * TILE
    edge_rows = group_hbm.shape[1] - rows
    first = jnp.where(low, REACH, 0)
    moves = [
        (group_hbm.at[first + part, pl.ds(0, rows)], half_out.at[pl.ds(part * rows, rows)])
        for part in range(REACH)
    ]
    moves.append(
        (
            group_hbm.at[jnp.where(low, GROUP - 1, 0), pl.ds(rows, edge_rows)],
            half_out.at[pl.ds(REACH * rows, edge_rows)],
        )
    )
    moves = fetch(moves, half_sems)
    for copy in copies:
        copy.wait()
    roots = [roots_v[peer] for peer in range(GROUP)]
    start, tiles = 0, []
    for level in range(1, DEPTH):
        width = 1 << level
        count = GROUP // width
        left = jnp.concatenate(
            [row_of(roots[n * width : (n + 1) * width]) for n in range(count)], axis=0
        )
        size = left.shape[1]
        nodes = dot_halves(left, up_high[start : start + size], up_low[start : start + size], NN)
        start += size
        tiles += [fold(nodes[n * 2 * TILE : (n + 1) * 2 * TILE]) for n in range(count)]
    row = REACH * rows + edge_rows
    for index, tile in enumerate(tiles):
        half_out[row + index * TILE : row + (index + 1) * TILE, :] = tile
        for peer in range(nodes_out.shape[0]):
            nodes_out[peer, index] = tile
    for index in range(3):
        far_out[index] = tiles[NODES - 3 + index]
    for copy in moves:
        copy.wait()


def down_kernel(parts, me_ref, *refs):
    node_parts, refs = refs[:parts], refs[parts:]
    count = (len(refs) - 5) // 2
    out_ref = refs[count]
    held = refs[count + 1 : 2 * count + 1]
    nodes_ref, y_tree, sems, node_sems = refs[2 * count + 1 :]
    me = me_ref[0]
    groups = nodes_ref.shape[0]
    group = lax.shift_right_logical(me, 3)
    place = me & (GROUP - 1)
    low = place < REACH
    if parts > 1:
        near_by, far_by = jnp.where(low, groups - 1, 1), jnp.where(low, 1, groups - 1)
        across = lax.rem(group + 2, groups)
        near_group = lax.rem(group + near_by, groups)
        node_copies = fetch(
            [
                (node_parts[0].at[0], nodes_ref.at[group]),
                (node_parts[1].at[0], nodes_ref.at[lax.rem(group + far_by, groups)]),
                (node_parts[2], nodes_ref.at[across, pl.ds(NODES - 3, 3)]),
            ],
            node_sems,
        )
    else:
        node_copies = fetch([(node_parts[0], nodes_ref)], node_sems)
    copies = fetch(list(zip(refs[:count], held)), sems)
    (
        group_ref,
        half_ref,
        far_ids_s,
        far_count_s,
        path_high,
        path_low,
        leaf_high,
        leaf_low,
        lift_high,
        lift_low,
        edge_high,
        edge_low,
        bases_high,
        bases_low,
        near_ref,
        inverse_ref,
    ) = held
    leaf_dev, vectors, leaf_size = near_ref.shape
    points_dev = out_ref.shape[1]
    slots = far_ids_s.shape[1]
    per_leaf = leaf_size // LANES
    rank = bases_high.shape[1] // 2
    start = (leaf_dev + 1) * TILE
    edge_rows = group_ref.shape[1] - start

    def tile_of(subtree, index):
        other = subtree & (GROUP - 1)
        inside = lax.shift_right_arithmetic(subtree, 3) == group
        row = pl.multiple_of(index * TILE, TILE)
        near_row = jnp.clip(other - jnp.where(low, REACH, 0), 0, REACH - 1) * start
        here = group_ref[other, pl.ds(row, TILE), :]
        there = half_ref[pl.ds(pl.multiple_of(near_row + row, TILE), TILE), :]
        return jnp.where(inside, here, there)

    for copy in node_copies + copies[:6]:
        copy.wait()
    if parts > 1:
        for index in range(NODES):
            row = half_ref.shape[0] - (NODES - index) * TILE
            tile = half_ref[row : row + TILE, :]
            nodes_ref[near_group, index] = tile
    partners = []
    for level in range(DEPTH):
        node = lax.shift_right_logical(me, level)
        size = (groups * GROUP) >> level
        for offset in OFFSETS:
            other = node + offset
            used = (other >= 0) & (other < size)
            other = jnp.clip(other, 0, size - 1)
            if level == 0:
                tile = tile_of(other, leaf_dev)
            else:
                shift = DEPTH - 1 - level
                first = GROUP - (2 << shift)
                tile = nodes_ref[
                    lax.shift_right_logical(other, shift), first + (other & ((1 << shift) - 1))
                ]
            partners.append(jnp.where(used, tile, 0.0))
    top = lax.shift_right_logical(me, DEPTH)
    for side in range(2):
        blended = jnp.zeros((TILE, LANES), F32)
        for other in range(groups // 2):
            distance = jnp.abs(top - other)
            weight = jnp.where(distance >= 2, 1.0 / jnp.maximum(distance, 1).astype(F32), 0.0)
            blended = blended + weight * nodes_ref[2 * other + side, GROUP - 2]
        partners.append(blended)
    half = len(partners) // 2
    row = row_of(partners)
    first, second = pair_dot(
        row[:, : half * rank], row[:, half * rank :], path_high[...], path_low[...]
    )
    down = first[:, :rank] + second[:, rank:]

    rows = []
    for leaf in range(leaf_dev):
        picked = []
        for slot in range(slots):
            used = slot < far_count_s[leaf]
            spot = far_ids_s[leaf, slot]
            tile = tile_of(lax.shift_right_logical(spot, 3), spot & (leaf_dev - 1))
            picked.append(jnp.where(used, tile, 0.0))
        rows.append(row_of(picked))
    edges = []
    for offset in (-1, 1):
        other = me + offset
        inside = lax.shift_right_arithmetic(other, 3) == group
        here = group_ref[other & (GROUP - 1), start:, :]
        chosen = jnp.where(inside, here, half_ref[REACH * start : REACH * start + edge_rows, :])
        edges.append(
            jnp.concatenate(
                [chosen[part * vectors : (part + 1) * vectors] for part in range(per_leaf)], axis=1
            )
        )

    for copy in copies[6:]:
        copy.wait()
    edge_parts = [
        dot_halves(edges[index], edge_high[index], edge_low[index], NN) for index in range(2)
    ]
    left_half = lax.broadcasted_iota(jnp.int32, (vectors, 2 * rank), 1) < rank
    for pair in range(leaf_dev // 2):
        two = (2 * pair, 2 * pair + 1)
        first, second = pair_dot(rows[two[0]], rows[two[1]], leaf_high[pair], leaf_low[pair])
        lift = dot_halves(down, lift_high[pair], lift_low[pair], NN)
        first = jnp.where(left_half, first + lift, 0.0)
        second = jnp.where(left_half, 0.0, second + lift)
        products = pair_dot(first, second, bases_high[pair], bases_low[pair])
        for leaf, product in zip(two, products):
            y_leaf = near_ref[leaf] + product
            if leaf == 0:
                y_leaf = y_leaf + edge_parts[0]
            if leaf == leaf_dev - 1:
                y_leaf = y_leaf + edge_parts[1]
            y_tree[:, leaf * leaf_size : (leaf + 1) * leaf_size] = y_leaf

    y = y_tree[...]
    for tile in range(points_dev // LANES):
        spot = inverse_ref[tile : tile + 1, :]
        out_ref[:, tile * LANES : (tile + 1) * LANES] = lane_gather(
            y, lax.shift_right_logical(spot, 7), spot & (LANES - 1)
        )


def local(
    devices,
    points,
    order,
    bases,
    lift,
    near_ids,
    near_blocks,
    far_ids,
    far_count,
    far_blocks,
    transfer,
    couple,
    links,
    top_couple,
):
    me = lax.axis_index("leaf").astype(jnp.int32).reshape(1)
    vectors, points_dev = points.shape
    leaf_dev, leaf_size, rank = bases.shape
    slots = near_ids.shape[1]
    far_slots = far_ids.shape[1]
    bases_t = jnp.swapaxes(bases, 1, 2)
    tiles = points_dev // LANES
    edge_rows = vectors * (leaf_size // LANES)
    rows = (leaf_dev + 1) * TILE
    groups = devices // GROUP
    order_tiles = order.reshape(tiles, LANES)
    shape = jax.ShapeDtypeStruct

    group_out, tree_x = pl.pallas_call(
        up_kernel,
        out_shape=[
            shape((GROUP, rows + edge_rows, LANES), F32),
            shape((leaf_dev, vectors, leaf_size), F32),
        ],
        in_specs=[SMEM] + [HBM] * 4,
        out_specs=[VMEM] * 2,
        scratch_shapes=[
            pltpu.VMEM(points.shape, F32),
            pltpu.VMEM((tiles, LANES), jnp.int32),
            pltpu.VMEM(bases_t.shape, F32),
            pltpu.VMEM(lift.shape, F32),
            pltpu.SemaphoreType.DMA((4,)),
        ],
        compiler_params=PARAMS,
        name="up",
    )(me, points, order_tiles, bases_t, lift)

    aligned = [[g * GROUP + i for i in range(GROUP)] for g in range(groups)]
    group_in = lax.all_to_all(group_out, "leaf", 0, 0, axis_index_groups=aligned, tiled=True)

    ids_t = near_ids.T
    both = lambda *size: [shape(size, BF16)] * 2

    links_own = links.reshape(links.shape[1:])
    path_rows = (DEPTH * len(OFFSETS) + 2) // 2 * rank
    operands = (
        ids_t,
        links_own,
        transfer,
        couple,
        tree_x,
        top_couple,
        lift,
        order.reshape(1, points_dev),
        far_blocks,
        bases_t.reshape(leaf_dev // 2, 2 * rank, leaf_size),
        near_blocks,
    )
    results = (
        both(14 * rank, rank)
        + both(path_rows, 2 * rank)
        + [shape((tiles, LANES), jnp.int32)]
        + both(leaf_dev // 2, far_slots * rank, 2 * rank)
        + both(leaf_dev // 2, rank, 2 * rank)
        + both(leaf_dev // 2, 2 * rank, leaf_size)
        + both(2, leaf_size, leaf_size)
        + [shape(tree_x.shape, F32)]
    )
    (
        up_high,
        up_low,
        path_high,
        path_low,
        inverse,
        leaf_high,
        leaf_low,
        lift_high,
        lift_low,
        bases_high,
        bases_low,
        edge_high,
        edge_low,
        near_part,
    ) = pl.pallas_call(
        side_kernel,
        out_shape=results,
        in_specs=[SMEM] + [HBM] * len(operands),
        out_specs=[HBM] * len(results),
        scratch_shapes=[
            (pltpu.SMEM if x is ids_t or x is links_own else pltpu.VMEM)(x.shape, x.dtype)
            for x in operands
        ]
        + [pltpu.VMEM(x.shape, x.dtype) for x in results]
        + [
            pltpu.SemaphoreType.DMA((10,)),
            pltpu.SemaphoreType.DMA((leaf_dev // 2,)),
            pltpu.SemaphoreType.DMA((len(results),)),
        ],
        compiler_params=PARAMS,
        cost_estimate=pl.CostEstimate(
            flops=250 * 12_000_000, bytes_accessed=12_000_000, transcendentals=0
        ),
        name="side",
    )(me, *operands)

    by_permute = groups == 4
    half_out, nodes_out, far_nodes = pl.pallas_call(
        functools.partial(middle_kernel, leaf_dev),
        out_shape=[
            shape((REACH * rows + edge_rows + NODES * TILE, LANES), F32),
            shape((1 if by_permute else groups, NODES, TILE, LANES), F32),
            shape((3, TILE, LANES), F32),
        ],
        in_specs=[SMEM] + [HBM] * 3,
        out_specs=[VMEM] * 3,
        scratch_shapes=[
            pltpu.VMEM((GROUP, TILE, LANES), F32),
            pltpu.VMEM(up_high.shape, BF16),
            pltpu.VMEM(up_low.shape, BF16),
            pltpu.SemaphoreType.DMA((3,)),
            pltpu.SemaphoreType.DMA((REACH + 1,)),
        ],
        compiler_params=PARAMS,
        name="middle",
    )(me, group_in, up_high, up_low)

    def shifted(x, low, high):
        pairs = []
        for device in range(devices):
            by = low if device % GROUP < REACH else high
            pairs.append(((device + by * GROUP) % devices, device))
        return lax.ppermute(x, "leaf", pairs)

    half_in = shifted(half_out, -1, 1)
    if by_permute:
        node_parts = (nodes_out, shifted(nodes_out, 1, -1), shifted(far_nodes, 2, 2))
    else:
        across = [[g * GROUP + i for g in range(groups)] for i in range(GROUP)]
        node_parts = (lax.all_to_all(nodes_out, "leaf", 0, 0, axis_index_groups=across, tiled=True),)

    operands = (
        group_in,
        half_in,
        far_ids,
        far_count,
        path_high,
        path_low,
        leaf_high,
        leaf_low,
        lift_high,
        lift_low,
        edge_high,
        edge_low,
        bases_high,
        bases_low,
        near_part,
        inverse,
    )
    return pl.pallas_call(
        functools.partial(down_kernel, len(node_parts)),
        out_shape=shape((vectors, points_dev), F32),
        in_specs=[SMEM] + [HBM] * (len(node_parts) + len(operands)),
        out_specs=VMEM,
        scratch_shapes=[
            (pltpu.SMEM if x is far_ids or x is far_count else pltpu.VMEM)(x.shape, x.dtype)
            for x in operands
        ]
        + [
            pltpu.VMEM((groups, NODES, TILE, LANES), F32),
            pltpu.VMEM((vectors, points_dev), F32),
            pltpu.SemaphoreType.DMA((len(operands),)),
            pltpu.SemaphoreType.DMA((3,)),
        ],
        compiler_params=PARAMS,
        name="down",
    )(me, *node_parts, *operands)


def solution(mesh):
    in_specs = (
        P(None, "leaf"),
        P("leaf"),
        P("leaf", None, None),
        P("leaf", None, None),
        P("leaf", None),
        P("leaf", None, None, None),
        P("leaf", None),
        P("leaf"),
        P("leaf", None, None, None),
        P(),
        P(),
        P("leaf", None, None),
        P(),
    )
    return jax.shard_map(
        functools.partial(local, mesh.shape["leaf"]),
        mesh=mesh,
        in_specs=in_specs,
        out_specs=P(None, "leaf"),
        check_vma=False,
    )
```

profile of v0, /device:TPU:0, one launch (start us, length us, event | category | flops | bytes accessed | tf_op | source)
XLA Modules:
  0.0 34.2 jit_solution(16984345155820179535)
XLA Ops:
  0.0 3.0 %up.1 = (f32[8,104,128]{2,1,0:T(8,128)}, f32[8,16,256]{2,1,0:T(8,128)}) custom-call(s32[1]{0:T(128)} %bitcast.me_ref, f32[16,2048]{1,0:T(8,128)} %points_hbm.1, s32[16,128]{1,0:T(8,128)} %bitcast.10, f32[8,64,256]{2,1,0:T(8,128)} %bitcast.8, f32[8,64,64]{2,1,0:T(8,128)} %refs_6_.2), custom_call_target="tpu_custom_call" | custom-call | tf_op jit(solution)/shard_map/up/pallas_call | solution.py:542
  3.0 5.2 %all-to-all-start = ((f32[8,104,128]{2,1,0:T(8,128)}), f32[8,104,128]{2,1,0:T(8,128)}, u32[]{:S(2)}, u32[]{:S(2)}) async-start(f32[8,104,128]{2,1,0:T(8,128)} %get-tuple-element.24), calls=%async_computation | async-start | bytes 851968 | tf_op jit(solution)/shard_map/all_to_all | solution.py:562
  8.2 8.0 %side.1 = (bf16[896,64]{1,0:T(8,128)(2,1)}, bf16[896,64]{1,0:T(8,128)(2,1)}, bf16[576,128]{1,0:T(8,128)(2,1)}, bf16[576,128]{1,0:T(8,128)(2,1)}, s32[16,128]{1,0...) custom-call(s32[1]{0:T(128)} %bitcast.me_ref, ...), custom_call_target="tpu_custom_call" | custom-call | flops 3000000000 | bytes 12000000 | tf_op jit(solution)/shard_map/side/pallas_call | solution.py:607
  16.2 0.8 %all-to-all-done.group_hbm.refs_3_ = f32[8,104,128]{2,1,0:T(8,128)} async-done(((f32[8,104,128]{2,1,0:T(8,128)}), f32[8,104,128]{2,1,0:T(8,128)}, u32[]{:S(2)}, u32[]{:S(2)}) %all-to-all-start) | async-done | bytes 426016 | tf_op jit(solution)/shard_map/all_to_all | solution.py:562
  17.0 2.2 %middle.1 = (f32[376,128]{1,0:T(8,128)}, f32[1,7,8,128]{3,2,1,0:T(8,128)}, f32[3,8,128]{2,1,0:T(8,128)}) custom-call(s32[1]{0:T(128)} %bitcast.me_ref, f32[8,104,128]{2,1,0:T(8,128)} %all-to-all-done.group_hbm.refs_3_, bf16[896,64]{1,0:T(8,128)(2,1)} %get-tuple-element.26.up_high_hbm, bf16[896,64]{1,0:T(8,128)(2,1)} %get-tuple-element.27.up_low_hbm), custom_call_target="tpu_custom_call" | custom-call | tf_op jit(solution)/shard_map/middle/pallas_call | solution.py:630
  19.2 1.9 %collective-permute-start.2 = (f32[376,128]{1,0:T(8,128)}, f32[376,128]{1,0:T(8,128)}, u32[]{:S(2)}, u32[]{:S(2)}) collective-permute-start(f32[376,128]{1,0:T(8,128)} %get-tuple-element.30), channel_id=1, source_target_pairs={{24,0},{25,1},{26,2},{27,3},{12,4},{13,5},{14,6},{15,7},{0,8},{1,9... | collective-permute-start | bytes 577544 | tf_op jit(solution)/shard_map/ppermute | solution.py:655
  21.1 2.1 %collective-permute-start = (f32[1,7,8,128]{3,2,1,0:T(8,128)}, f32[1,7,8,128]{3,2,1,0:T(8,128)}, u32[]{:S(2)}, u32[]{:S(2)}) collective-permute-start(f32[1,7,8,128]{3,2,1,0:T(8,128)} %get-tuple-element.28.refs_0_), channel_id=1, source_target_pairs={{8,0},{9,1},{10,2},{11,3},{28,4},{29,5},{30,6},{31,7},{16,8},{17,9... | collective-permute-start | bytes 86024 | tf_op jit(solution)/shard_map/ppermute | solution.py:655
  23.2 0.9 %collective-permute-start.1 = (f32[3,8,128]{2,1,0:T(8,128)}, f32[3,8,128]{2,1,0:T(8,128)}, u32[]{:S(2)}, u32[]{:S(2)}) collective-permute-start(f32[3,8,128]{2,1,0:T(8,128)} %get-tuple-element.29), channel_id=1, source_target_pairs={{16,0},{17,1},{18,2},{19,3},{20,4},{21,5},{22,6},{23,7},{24,8},{25... | collective-permute-start | bytes 36872 | tf_op jit(solution)/shard_map/ppermute | solution.py:655
  24.2 5.1 %collective-permute-done.1.refs_2_ = f32[3,8,128]{2,1,0:T(8,128)} collective-permute-done((f32[3,8,128]{2,1,0:T(8,128)}, f32[3,8,128]{2,1,0:T(8,128)}, u32[]{:S(2)}, u32[]{:S(2)}) %collective-permute-start.1) | collective-permute-done | bytes 12320 | tf_op jit(solution)/shard_map/ppermute | solution.py:655
  29.3 0.0 collective-permute-done.refs_1_
  29.3 0.0 collective-permute-done.2.refs_4_
  29.3 4.8 %down.1 = f32[16,2048]{1,0:T(8,128)} custom-call(s32[1]{0:T(128)} %bitcast.me_ref, f32[1,7,8,128]{3,2,1,0:T(8,128)} %get-tuple-element.28.refs_0_, f32[1,7,8,128]{3,2,1,0:T(8,128)} %collective-permute-done.refs_1_, f32[3,8,128]{2,1,0:T(8,128)} %collective-permute-done.1.refs_2_, f32[8,104,128]{2,1,0:T(8,128)} %all-to-all-done.group_hbm.refs_3_, ...), custom_call_target="tpu_custom_call" | custom-call | tf_op jit(solution)/shard_map/down/pallas_call | solution.py:682
Async XLA Ops:
  3.0 14.0 %all-to-all-start = ((f32[8,104,128]{2,1,0:T(8,128)}), f32[8,104,128]{2,1,0:T(8,128)}, u32[]{:S(2)}, u32[]{:S(2)}) async-start(f32[8,104,128]{2,1,0:T(8,128)} %get-tuple-element.24), calls=%async_computation | async-start | bytes 851968 | tf_op jit(solution)/shard_map/all_to_all | solution.py:562
  19.2 10.1 %collective-permute-start.2 = (f32[376,128]{1,0:T(8,128)}, f32[376,128]{1,0:T(8,128)}, u32[]{:S(2)}, u32[]{:S(2)}) collective-permute-start(f32[376,128]{1,0:T(8,128)} %get-tuple-element.30), channel_id=1, source_target_pairs={{24,0},{25,1},{26,2},{27,3},{12,4},{13,5},{14,6},{15,7},{0,8},{1,9... | collective-permute-start | bytes 577544 | tf_op jit(solution)/shard_map/ppermute | solution.py:655
  21.1 8.2 %collective-permute-start = (f32[1,7,8,128]{3,2,1,0:T(8,128)}, f32[1,7,8,128]{3,2,1,0:T(8,128)}, u32[]{:S(2)}, u32[]{:S(2)}) collective-permute-start(f32[1,7,8,128]{3,2,1,0:T(8,128)} %get-tuple-element.28.refs_0_), channel_id=1, source_target_pairs={{8,0},{9,1},{10,2},{11,3},{28,4},{29,5},{30,6},{31,7},{16,8},{17,9... | collective-permute-start | bytes 86024 | tf_op jit(solution)/shard_map/ppermute | solution.py:655
  23.2 6.1 %collective-permute-start.1 = (f32[3,8,128]{2,1,0:T(8,128)}, f32[3,8,128]{2,1,0:T(8,128)}, u32[]{:S(2)}, u32[]{:S(2)}) collective-permute-start(f32[3,8,128]{2,1,0:T(8,128)} %get-tuple-element.29), channel_id=1, source_target_pairs={{16,0},{17,1},{18,2},{19,3},{20,4},{21,5},{22,6},{23,7},{24,8},{25... | collective-permute-start | bytes 36872 | tf_op jit(solution)/shard_map/ppermute | solution.py:655
where the time goes:
time: 34.4 us; the launch traced here: 34.2 us
  Pallas kernels  18.1 us (53%)
  starting transfers between devices  10.1 us (29%)
  waiting for transfers between devices  5.92 us (17%)
    pallas_call x1, Pallas kernels, local(): pl.pallas_call(side_kernel, out_shape=results, in_specs=[SMEM] + [HBM] *...  8.02 us
    all_to_all x1, starting transfers between devices, local(): lax.all_to_all(group_out, 'leaf', 0, 0, axis_index_groups=aligned, tiled=...  5.19 us
    ppermute x3, waiting for transfers between devices, shifted(): return lax.ppermute(x, 'leaf', pairs)  5.15 us
    ppermute x3, starting transfers between devices, shifted(): return lax.ppermute(x, 'leaf', pairs)  4.96 us
    pallas_call x1, Pallas kernels, local(): pl.pallas_call(functools.partial(down_kernel, len(node_parts)), out_shape...  4.84 us
    pallas_call x1, Pallas kernels, local(): pl.pallas_call(up_kernel, out_shape=[shape((GROUP, rows + edge_rows, LANE...  2.99 us
    pallas_call x1, Pallas kernels, local(): pl.pallas_call(functools.partial(middle_kernel, leaf_dev), out_shape=[sha...  2.23 us
    all_to_all x1, waiting for transfers between devices, local(): lax.all_to_all(group_out, 'leaf', 0, 0, axis_index_groups=aligned, tiled=...  0.77 us
  transfers between devices with their start and end apart: 4, of which 2 were waited for; matrix products, arithmetic and copies ran while one was open for 0% of the time, Pallas kernels for 23%

commit v1 on v0

--- a/solution.py
+++ b/solution.py
@@ -303,7 +303,8 @@
     group_hbm,
     up_high_hbm,
     up_low_hbm,
-    half_out,
+    near_half,
+    far_half,
     nodes_out,
     far_out,
     roots_v,
@@ -323,15 +324,19 @@
     )
     rows = (leaf_dev + 1) * TILE
     edge_rows = group_hbm.shape[1] - rows
-    first = jnp.where(low, REACH, 0)
+    count = REACH // 2
     moves = [
-        (group_hbm.at[first + part, pl.ds(0, rows)], half_out.at[pl.ds(part * rows, rows)])
-        for part in range(REACH)
+        (group_hbm.at[first + part, pl.ds(0, rows)], half.at[pl.ds(part * rows, rows)])
+        for half, first in (
+            (near_half, jnp.where(low, GROUP - count, 0)),
+            (far_half, jnp.where(low, count, REACH)),
+        )
+        for part in range(count)
     ]
     moves.append(
         (
             group_hbm.at[jnp.where(low, GROUP - 1, 0), pl.ds(rows, edge_rows)],
-            half_out.at[pl.ds(REACH * rows, edge_rows)],
+            near_half.at[pl.ds(count * rows, edge_rows)],
         )
     )
     moves = fetch(moves, half_sems)
@@ -341,17 +346,17 @@
     start, tiles = 0, []
     for level in range(1, DEPTH):
         width = 1 << level
-        count = GROUP // width
+        some = GROUP // width
         left = jnp.concatenate(
-            [row_of(roots[n * width : (n + 1) * width]) for n in range(count)], axis=0
+            [row_of(roots[n * width : (n + 1) * width]) for n in range(some)], axis=0
         )
         size = left.shape[1]
         nodes = dot_halves(left, up_high[start : start + size], up_low[start : start + size], NN)
         start += size
-        tiles += [fold(nodes[n * 2 * TILE : (n + 1) * 2 * TILE]) for n in range(count)]
-    row = REACH * rows + edge_rows
+        tiles += [fold(nodes[n * 2 * TILE : (n + 1) * 2 * TILE]) for n in range(some)]
+    row = count * rows + edge_rows
     for index, tile in enumerate(tiles):
-        half_out[row + index * TILE : row + (index + 1) * TILE, :] = tile
+        near_half[row + index * TILE : row + (index + 1) * TILE, :] = tile
         for peer in range(nodes_out.shape[0]):
             nodes_out[peer, index] = tile
     for index in range(3):
@@ -361,11 +366,11 @@
 
 
 def down_kernel(parts, me_ref, *refs):
-    node_parts, refs = refs[:parts], refs[parts:]
-    count = (len(refs) - 5) // 2
+    halves_hbm, node_parts, refs = refs[:2], refs[2 : 2 + parts], refs[2 + parts :]
+    count = (len(refs) - 7) // 2
     out_ref = refs[count]
     held = refs[count + 1 : 2 * count + 1]
-    nodes_ref, y_tree, sems, node_sems = refs[2 * count + 1 :]
+    nodes_ref, half_ref, y_tree, sems, node_sems, half_sems = refs[2 * count + 1 :]
     me = me_ref[0]
     groups = nodes_ref.shape[0]
     group = lax.shift_right_logical(me, 3)
@@ -385,10 +390,20 @@
         )
     else:
         node_copies = fetch([(node_parts[0], nodes_ref)], node_sems)
+    quarter = halves_hbm[1].shape[0]
+    near_start = pl.multiple_of(jnp.where(low, quarter, 0), TILE)
+    rest = halves_hbm[0].shape[0] - quarter
+    node_copies += fetch(
+        [
+            (halves_hbm[0].at[pl.ds(0, quarter)], half_ref.at[pl.ds(near_start, quarter)]),
+            (halves_hbm[1], half_ref.at[pl.ds(pl.multiple_of(quarter - near_start, TILE), quarter)]),
+            (halves_hbm[0].at[pl.ds(quarter, rest)], half_ref.at[pl.ds(2 * quarter, rest)]),
+        ],
+        half_sems,
+    )
     copies = fetch(list(zip(refs[:count], held)), sems)
     (
         group_ref,
-        half_ref,
         far_ids_s,
         far_count_s,
         path_high,
@@ -421,7 +436,7 @@
         there = half_ref[pl.ds(pl.multiple_of(near_row + row, TILE), TILE), :]
         return jnp.where(inside, here, there)
 
-    for copy in node_copies + copies[:6]:
+    for copy in node_copies + copies[:5]:
         copy.wait()
     if parts > 1:
         for index in range(NODES):
@@ -481,7 +496,7 @@
             )
         )
 
-    for copy in copies[6:]:
+    for copy in copies[5:]:
         copy.wait()
     edge_parts = [
         dot_halves(edges[index], edge_high[index], edge_low[index], NN) for index in range(2)
@@ -627,15 +642,16 @@
     )(me, *operands)
 
     by_permute = groups == 4
-    half_out, nodes_out, far_nodes = pl.pallas_call(
+    near_half, far_half, nodes_out, far_nodes = pl.pallas_call(
         functools.partial(middle_kernel, leaf_dev),
         out_shape=[
-            shape((REACH * rows + edge_rows + NODES * TILE, LANES), F32),
+            shape((REACH // 2 * rows + edge_rows + NODES * TILE, LANES), F32),
+            shape((REACH // 2 * rows, LANES), F32),
             shape((1 if by_permute else groups, NODES, TILE, LANES), F32),
             shape((3, TILE, LANES), F32),
         ],
         in_specs=[SMEM] + [HBM] * 3,
-        out_specs=[VMEM] * 3,
+        out_specs=[VMEM] * 4,
         scratch_shapes=[
             pltpu.VMEM((GROUP, TILE, LANES), F32),
             pltpu.VMEM(up_high.shape, BF16),
@@ -654,7 +670,13 @@
             pairs.append(((device + by * GROUP) % devices, device))
         return lax.ppermute(x, "leaf", pairs)
 
-    half_in = shifted(half_out, -1, 1)
+    half_in = shifted(near_half, -1, 1)
+    pairs = []
+    for device in range(devices):
+        side = -1 if device % GROUP < REACH else 1
+        if 0 <= device // GROUP + side < groups:
+            pairs.append((device + side * (GROUP - REACH), device))
+    quarter_in = lax.ppermute(far_half, "leaf", pairs)
     if by_permute:
         node_parts = (nodes_out, shifted(nodes_out, 1, -1), shifted(far_nodes, 2, 2))
     else:
@@ -663,7 +685,6 @@
 
     operands = (
         group_in,
-        half_in,
         far_ids,
         far_count,
         path_high,
@@ -682,7 +703,7 @@
     return pl.pallas_call(
         functools.partial(down_kernel, len(node_parts)),
         out_shape=shape((vectors, points_dev), F32),
-        in_specs=[SMEM] + [HBM] * (len(node_parts) + len(operands)),
+        in_specs=[SMEM] + [HBM] * (2 + len(node_parts) + len(operands)),
         out_specs=VMEM,
         scratch_shapes=[
             (pltpu.SMEM if x is far_ids or x is far_count else pltpu.VMEM)(x.shape, x.dtype)
@@ -690,13 +711,15 @@
         ]
         + [
             pltpu.VMEM((groups, NODES, TILE, LANES), F32),
+            pltpu.VMEM((half_in.shape[0] + quarter_in.shape[0], LANES), F32),
             pltpu.VMEM((vectors, points_dev), F32),
             pltpu.SemaphoreType.DMA((len(operands),)),
             pltpu.SemaphoreType.DMA((3,)),
+            pltpu.SemaphoreType.DMA((3,)),
         ],
         compiler_params=PARAMS,
         name="down",
-    )(me, *node_parts, *operands)
+    )(me, half_in, quarter_in, *node_parts, *operands)
 
 
 def solution(mesh):

time: 34.4 us -> 36.9 us (1.073)
  starting transfers between devices: 10.1 us -> 15.3 us
  waiting for transfers between devices: 5.92 us -> 3.1 us
    ppermute x3, starting transfers between devices: 4.96 us -> 8.8 us  [shifted(): return lax.ppermute(x, 'leaf', pairs)]
    ppermute x3, waiting for transfers between devices: 5.15 us -> 2.32 us  [shifted(): return lax.ppermute(x, 'leaf', pairs)]
    ppermute x0 -> x1, starting transfers between devices: none -> 1.29 us  [local(): quarter_in = lax.ppermute(far_half, 'leaf', pairs)]
  transfers between devices with their start and end apart: 4 -> 5, of which waited for: 2 -> 2; matrix products, arithmetic and copies ran while one was open for 0% -> 0% of each run, Pallas kernels for 23% -> 22%
where the time goes in v1:
time: 36.9 us; the launch traced here: 36.6 us
  Pallas kernels  18.2 us (49%)
  starting transfers between devices  15.3 us (41%)
  waiting for transfers between devices  3.1 us (8%)
    ppermute x3, starting transfers between devices, shifted(): return lax.ppermute(x, 'leaf', pairs)  8.8 us
    pallas_call x1, Pallas kernels, local(): pl.pallas_call(side_kernel, out_shape=results, in_specs=[SMEM] + [HBM] *...  8.01 us
    all_to_all x1, starting transfers between devices, local(): lax.all_to_all(group_out, 'leaf', 0, 0, axis_index_groups=aligned, tiled=...  5.19 us
    pallas_call x1, Pallas kernels, local(): pl.pallas_call(functools.partial(down_kernel, len(node_parts)), out_shape...  4.96 us
    pallas_call x1, Pallas kernels, local(): pl.pallas_call(up_kernel, out_shape=[shape((GROUP, rows + edge_rows, LANE...  2.99 us
    ppermute x3, waiting for transfers between devices, shifted(): return lax.ppermute(x, 'leaf', pairs)  2.32 us
    pallas_call x1, Pallas kernels, local(): pl.pallas_call(functools.partial(middle_kernel, leaf_dev), out_shape=[sha...  2.22 us
    ppermute x1, starting transfers between devices, local(): quarter_in = lax.ppermute(far_half, 'leaf', pairs)  1.29 us
  transfers between devices with their start and end apart: 5, of which 2 were waited for; matrix products, arithmetic and copies ran while one was open for 0% of the time, Pallas kernels for 22%

profile of v1, /device:TPU:0, one launch (start us, length us, event | category | flops | bytes accessed | tf_op | source)
XLA Modules:
  0.0 36.6 jit_solution(765745391030123730)
XLA Ops:
  0.0 3.0 %up.1 = (f32[8,104,128]{2,1,0:T(8,128)}, f32[8,16,256]{2,1,0:T(8,128)}) custom-call(s32[1]{0:T(128)} %bitcast.me_ref, f32[16,2048]{1,0:T(8,128)} %points_hbm.1, s32[16,128]{1,0:T(8,128)} %bitcast.10, f32[8,64,256]{2,1,0:T(8,128)} %bitcast.8, f32[8,64,64]{2,1,0:T(8,128)} %refs_6_.2), custom_call_target="tpu_custom_call" | custom-call | tf_op jit(solution)/shard_map/up/pallas_call | solution.py:557
  3.0 5.2 %all-to-all-start = ((f32[8,104,128]{2,1,0:T(8,128)}), f32[8,104,128]{2,1,0:T(8,128)}, u32[]{:S(2)}, u32[]{:S(2)}) async-start(f32[8,104,128]{2,1,0:T(8,128)} %get-tuple-element.25), calls=%async_computation | async-start | bytes 851968 | tf_op jit(solution)/shard_map/all_to_all | solution.py:577
  8.2 8.0 %side.1 = (bf16[896,64]{1,0:T(8,128)(2,1)}, bf16[896,64]{1,0:T(8,128)(2,1)}, bf16[576,128]{1,0:T(8,128)(2,1)}, bf16[576,128]{1,0:T(8,128)(2,1)}, s32[16,128]{1,0...) custom-call(s32[1]{0:T(128)} %bitcast.me_ref, ...), custom_call_target="tpu_custom_call" | custom-call | flops 3000000000 | bytes 12000000 | tf_op jit(solution)/shard_map/side/pallas_call | solution.py:622
  16.2 0.8 %all-to-all-done.group_hbm.refs_5_ = f32[8,104,128]{2,1,0:T(8,128)} async-done(((f32[8,104,128]{2,1,0:T(8,128)}), f32[8,104,128]{2,1,0:T(8,128)}, u32[]{:S(2)}, u32[]{:S(2)}) %all-to-all-start) | async-done | bytes 426016 | tf_op jit(solution)/shard_map/all_to_all | solution.py:577
  17.0 2.2 %middle.1 = (f32[232,128]{1,0:T(8,128)}, f32[144,128]{1,0:T(8,128)}, f32[1,7,8,128]{3,2,1,0:T(8,128)}, f32[3,8,128]{2,1,0:T(8,128)}) custom-call(s32[1]{0:T(128)} %bitcast.me_ref, f32[8,104,128]{2,1,0:T(8,128)} %all-to-all-done.group_hbm.refs_5_, bf16[896,64]{1,0:T(8,128)(2,1)} %get-tuple-element.27.up_high_hbm, bf16[896,64]{1,0:T(8,128)(2,1)} %get-tuple-element.28.up_low_hbm), custom_call_target="tpu_custom_call" | custom-call | tf_op jit(solution)/shard_map/middle/pallas_call | solution.py:645
  19.2 1.9 %collective-permute-start = (f32[232,128]{1,0:T(8,128)}, f32[232,128]{1,0:T(8,128)}, u32[]{:S(2)}, u32[]{:S(2)}) collective-permute-start(f32[232,128]{1,0:T(8,128)} %get-tuple-element.29), channel_id=1, source_target_pairs={{24,0},{25,1},{26,2},{27,3},{12,4},{13,5},{14,6},{15,7},{0,8},{1,9... | collective-permute-start | bytes 356360 | tf_op jit(solution)/shard_map/ppermute | solution.py:671
  21.1 1.3 %collective-permute-start.1 = (f32[144,128]{1,0:T(8,128)}, f32[144,128]{1,0:T(8,128)}, u32[]{:S(2)}, u32[]{:S(2)}) collective-permute-start(f32[144,128]{1,0:T(8,128)} %get-tuple-element.30), channel_id=1, source_target_pairs={{8,4},{9,5},{10,6},{11,7},{4,8},{5,9},{6,10},{7,11},{16,12},{17,13... | collective-permute-start | bytes 221192 | tf_op jit(solution)/shard_map/ppermute | solution.py:679
  22.4 4.3 %collective-permute-start.2 = (f32[1,7,8,128]{3,2,1,0:T(8,128)}, f32[1,7,8,128]{3,2,1,0:T(8,128)}, u32[]{:S(2)}, u32[]{:S(2)}) collective-permute-start(f32[1,7,8,128]{3,2,1,0:T(8,128)} %get-tuple-element.31.refs_2_), channel_id=1, source_target_pairs={{8,0},{9,1},{10,2},{11,3},{28,4},{29,5},{30,6},{31,7},{16,8},{17,9... | collective-permute-start | bytes 86024 | tf_op jit(solution)/shard_map/ppermute | solution.py:671
  26.7 2.6 %collective-permute-start.3 = (f32[3,8,128]{2,1,0:T(8,128)}, f32[3,8,128]{2,1,0:T(8,128)}, u32[]{:S(2)}, u32[]{:S(2)}) collective-permute-start(f32[3,8,128]{2,1,0:T(8,128)} %get-tuple-element.32), channel_id=1, source_target_pairs={{16,0},{17,1},{18,2},{19,3},{20,4},{21,5},{22,6},{23,7},{24,8},{25... | collective-permute-start | bytes 36872 | tf_op jit(solution)/shard_map/ppermute | solution.py:671
  29.3 2.3 %collective-permute-done.3.refs_4_ = f32[3,8,128]{2,1,0:T(8,128)} collective-permute-done((f32[3,8,128]{2,1,0:T(8,128)}, f32[3,8,128]{2,1,0:T(8,128)}, u32[]{:S(2)}, u32[]{:S(2)}) %collective-permute-start.3) | collective-permute-done | bytes 12320 | tf_op jit(solution)/shard_map/ppermute | solution.py:671
  31.6 0.0 collective-permute-done.2.refs_3_
  31.6 0.0 collective-permute-done.1.refs_1_
  31.6 0.0 collective-permute-done.refs_0_
  31.6 5.0 %down.1 = f32[16,2048]{1,0:T(8,128)} custom-call(s32[1]{0:T(128)} %bitcast.me_ref, f32[232,128]{1,0:T(8,128)} %collective-permute-done.refs_0_, f32[144,128]{1,0:T(8,128)} %collective-permute-done.1.refs_1_, f32[1,7,8,128]{3,2,1,0:T(8,128)} %get-tuple-element.31.refs_2_, f32[1,7,8,128]{3,2,1,0:T(8,128)} %collective-permute-done.2.refs_3_, ...), custom_call_target="tpu_custom_call" | custom-call | tf_op jit(solution)/shard_map/down/pallas_call | solution.py:703
Async XLA Ops:
  3.0 14.0 %all-to-all-start = ((f32[8,104,128]{2,1,0:T(8,128)}), f32[8,104,128]{2,1,0:T(8,128)}, u32[]{:S(2)}, u32[]{:S(2)}) async-start(f32[8,104,128]{2,1,0:T(8,128)} %get-tuple-element.25), calls=%async_computation | async-start | bytes 851968 | tf_op jit(solution)/shard_map/all_to_all | solution.py:577
  19.2 12.4 %collective-permute-start = (f32[232,128]{1,0:T(8,128)}, f32[232,128]{1,0:T(8,128)}, u32[]{:S(2)}, u32[]{:S(2)}) collective-permute-start(f32[232,128]{1,0:T(8,128)} %get-tuple-element.29), channel_id=1, source_target_pairs={{24,0},{25,1},{26,2},{27,3},{12,4},{13,5},{14,6},{15,7},{0,8},{1,9... | collective-permute-start | bytes 356360 | tf_op jit(solution)/shard_map/ppermute | solution.py:671
  21.1 10.5 %collective-permute-start.1 = (f32[144,128]{1,0:T(8,128)}, f32[144,128]{1,0:T(8,128)}, u32[]{:S(2)}, u32[]{:S(2)}) collective-permute-start(f32[144,128]{1,0:T(8,128)} %get-tuple-element.30), channel_id=1, source_target_pairs={{8,4},{9,5},{10,6},{11,7},{4,8},{5,9},{6,10},{7,11},{16,12},{17,13... | collective-permute-start | bytes 221192 | tf_op jit(solution)/shard_map/ppermute | solution.py:679
  22.4 9.2 %collective-permute-start.2 = (f32[1,7,8,128]{3,2,1,0:T(8,128)}, f32[1,7,8,128]{3,2,1,0:T(8,128)}, u32[]{:S(2)}, u32[]{:S(2)}) collective-permute-start(f32[1,7,8,128]{3,2,1,0:T(8,128)} %get-tuple-element.31.refs_2_), channel_id=1, source_target_pairs={{8,0},{9,1},{10,2},{11,3},{28,4},{29,5},{30,6},{31,7},{16,8},{17,9... | collective-permute-start | bytes 86024 | tf_op jit(solution)/shard_map/ppermute | solution.py:671
  26.7 4.9 %collective-permute-start.3 = (f32[3,8,128]{2,1,0:T(8,128)}, f32[3,8,128]{2,1,0:T(8,128)}, u32[]{:S(2)}, u32[]{:S(2)}) collective-permute-start(f32[3,8,128]{2,1,0:T(8,128)} %get-tuple-element.32), channel_id=1, source_target_pairs={{16,0},{17,1},{18,2},{19,3},{20,4},{21,5},{22,6},{23,7},{24,8},{25... | collective-permute-start | bytes 36872 | tf_op jit(solution)/shard_map/ppermute | solution.py:671

commit v2 on v0

--- a/solution.py
+++ b/solution.py
@@ -107,10 +107,27 @@
 
 
 def up_kernel(
-    me_ref, points_hbm, order_hbm, bases_hbm, lift_hbm, out, x_out, points_v, order_v, bases_v, lift_v, sems
+    me_ref,
+    points_hbm,
+    order_hbm,
+    bases_hbm,
+    lift_hbm,
+    out_hbm,
+    x_hbm,
+    points_v,
+    order_v,
+    bases_v,
+    lift_v,
+    x_v,
+    tiles_v,
+    edges_v,
+    sems,
+    edge_sems,
+    tile_sems,
 ):
     copies = fetch(
-        [(order_hbm, order_v), (points_hbm, points_v), (bases_hbm, bases_v), (lift_hbm, lift_v)], sems
+        [(order_hbm, order_v), (points_hbm, points_v), (bases_hbm, bases_v), (lift_hbm, lift_v)],
+        sems,
     )
     me = me_ref[0]
     leaf_dev, rank, leaf_size = bases_v.shape
@@ -122,27 +139,39 @@
     for t in range(points_dev // LANES):
         spot = order_v[t : t + 1, :] - me * points_dev
         column = t % per_leaf * LANES
-        x_out[t // per_leaf, :, column : column + LANES] = lane_gather(
+        x_v[t // per_leaf, :, column : column + LANES] = lane_gather(
             points, lax.shift_right_logical(spot, 7), spot & (LANES - 1)
         )
+    for index, leaf in enumerate((0, leaf_dev - 1)):
+        for part in range(per_leaf):
+            edges_v[index, part * vectors : (part + 1) * vectors, :] = x_v[
+                leaf, :, part * LANES : (part + 1) * LANES
+            ]
+    rows = tiles_v.shape[0]
+    above = lax.rem(me + 1, GROUP)
+    writes = fetch([(x_v, x_hbm)], sems.at[pl.ds(4, 1)])
+    writes += fetch(
+        [
+            (
+                edges_v.at[jnp.where(above == peer, 1, 0)],
+                out_hbm.at[peer, pl.ds(rows, edges_v.shape[1])],
+            )
+            for peer in range(GROUP)
+        ],
+        edge_sems,
+    )
     copies[2].wait()
-    coefs = [dot3(x_out[leaf], bases_v[leaf], NT) for leaf in range(leaf_dev)]
-    tiles = [fold(coef) for coef in coefs]
+    coefs = [dot3(x_v[leaf], bases_v[leaf], NT) for leaf in range(leaf_dev)]
     copies[3].wait()
     weights = lift_v[...].reshape(leaf_dev * rank, rank)
-    tiles.append(fold(dot3(jnp.concatenate(coefs, axis=1), weights, NN)))
-    for peer in range(GROUP):
-        for index, tile in enumerate(tiles):
-            out[peer, index * TILE : (index + 1) * TILE, :] = tile
-    place = lax.rem(me, GROUP)
-    start = len(tiles) * TILE
-    for part in range(per_leaf):
-        first = x_out[0, :, part * LANES : (part + 1) * LANES]
-        last = x_out[leaf_dev - 1, :, part * LANES : (part + 1) * LANES]
-        rows = slice(start + part * vectors, start + (part + 1) * vectors)
-        for peer in range(GROUP):
-            above = lax.rem(place + 1, GROUP) == peer
-            out[peer, rows, :] = jnp.where(above, last, first)
+    root = dot3(jnp.concatenate(coefs, axis=1), weights, NN)
+    for index, matrix in enumerate(coefs + [root]):
+        tiles_v[index * TILE : (index + 1) * TILE, :] = fold(matrix)
+    writes += fetch(
+        [(tiles_v, out_hbm.at[peer, pl.ds(0, rows)]) for peer in range(GROUP)], tile_sems
+    )
+    for copy in writes:
+        copy.wait()
 
 
 def side_kernel(me_ref, *refs):
@@ -303,14 +332,16 @@
     group_hbm,
     up_high_hbm,
     up_low_hbm,
-    half_out,
+    half_hbm,
     nodes_out,
     far_out,
     roots_v,
     up_high,
     up_low,
+    half_out,
     sems,
     half_sems,
+    out_sems,
 ):
     low = lax.rem(me_ref[0], GROUP) < REACH
     copies = fetch(
@@ -335,8 +366,10 @@
         )
     )
     moves = fetch(moves, half_sems)
-    for copy in copies:
+    for copy in moves + copies:
         copy.wait()
+    row = REACH * rows + edge_rows
+    writes = fetch([(half_out.at[pl.ds(0, row)], half_hbm.at[pl.ds(0, row)])], out_sems)
     roots = [roots_v[peer] for peer in range(GROUP)]
     start, tiles = 0, []
     for level in range(1, DEPTH):
@@ -349,23 +382,24 @@
         nodes = dot_halves(left, up_high[start : start + size], up_low[start : start + size], NN)
         start += size
         tiles += [fold(nodes[n * 2 * TILE : (n + 1) * 2 * TILE]) for n in range(count)]
-    row = REACH * rows + edge_rows
     for index, tile in enumerate(tiles):
         half_out[row + index * TILE : row + (index + 1) * TILE, :] = tile
         for peer in range(nodes_out.shape[0]):
             nodes_out[peer, index] = tile
     for index in range(3):
         far_out[index] = tiles[NODES - 3 + index]
-    for copy in moves:
+    span = pl.ds(row, NODES * TILE)
+    writes += fetch([(half_out.at[span], half_hbm.at[span])], out_sems.at[pl.ds(1, 1)])
+    for copy in writes:
         copy.wait()
 
 
 def down_kernel(parts, me_ref, *refs):
     node_parts, refs = refs[:parts], refs[parts:]
-    count = (len(refs) - 5) // 2
+    count = (len(refs) - 7) // 2
     out_ref = refs[count]
     held = refs[count + 1 : 2 * count + 1]
-    nodes_ref, y_tree, sems, node_sems = refs[2 * count + 1 :]
+    nodes_ref, y_tree, out_v, sems, node_sems, out_sems = refs[2 * count + 1 :]
     me = me_ref[0]
     groups = nodes_ref.shape[0]
     group = lax.shift_right_logical(me, 3)
@@ -503,11 +537,19 @@
             y_tree[:, leaf * leaf_size : (leaf + 1) * leaf_size] = y_leaf
 
     y = y_tree[...]
-    for tile in range(points_dev // LANES):
+    writes = []
+    tiles = points_dev // LANES
+    for tile in range(tiles):
         spot = inverse_ref[tile : tile + 1, :]
-        out_ref[:, tile * LANES : (tile + 1) * LANES] = lane_gather(
+        out_v[:, tile * LANES : (tile + 1) * LANES] = lane_gather(
             y, lax.shift_right_logical(spot, 7), spot & (LANES - 1)
         )
+        if (tile + 1) % (tiles // 4) == 0:
+            span = pl.ds((tile + 1 - tiles // 4) * LANES, tiles // 4 * LANES)
+            sem = out_sems.at[pl.ds(len(writes), 1)]
+            writes += fetch([(out_v.at[:, span], out_ref.at[:, span])], sem)
+    for copy in writes:
+        copy.wait()
 
 
 def local(
@@ -546,13 +588,18 @@
             shape((leaf_dev, vectors, leaf_size), F32),
         ],
         in_specs=[SMEM] + [HBM] * 4,
-        out_specs=[VMEM] * 2,
+        out_specs=[HBM] * 2,
         scratch_shapes=[
             pltpu.VMEM(points.shape, F32),
             pltpu.VMEM((tiles, LANES), jnp.int32),
             pltpu.VMEM(bases_t.shape, F32),
             pltpu.VMEM(lift.shape, F32),
-            pltpu.SemaphoreType.DMA((4,)),
+            pltpu.VMEM((leaf_dev, vectors, leaf_size), F32),
+            pltpu.VMEM((rows, LANES), F32),
+            pltpu.VMEM((2, edge_rows, LANES), F32),
+            pltpu.SemaphoreType.DMA((5,)),
+            pltpu.SemaphoreType.DMA((GROUP,)),
+            pltpu.SemaphoreType.DMA((GROUP,)),
         ],
         compiler_params=PARAMS,
         name="up",
@@ -635,13 +682,15 @@
             shape((3, TILE, LANES), F32),
         ],
         in_specs=[SMEM] + [HBM] * 3,
-        out_specs=[VMEM] * 3,
+        out_specs=[HBM, VMEM, VMEM],
         scratch_shapes=[
             pltpu.VMEM((GROUP, TILE, LANES), F32),
             pltpu.VMEM(up_high.shape, BF16),
             pltpu.VMEM(up_low.shape, BF16),
+            pltpu.VMEM((REACH * rows + edge_rows + NODES * TILE, LANES), F32),
             pltpu.SemaphoreType.DMA((3,)),
             pltpu.SemaphoreType.DMA((REACH + 1,)),
+            pltpu.SemaphoreType.DMA((2,)),
         ],
         compiler_params=PARAMS,
         name="middle",
@@ -683,7 +732,7 @@
         functools.partial(down_kernel, len(node_parts)),
         out_shape=shape((vectors, points_dev), F32),
         in_specs=[SMEM] + [HBM] * (len(node_parts) + len(operands)),
-        out_specs=VMEM,
+        out_specs=HBM,
         scratch_shapes=[
             (pltpu.SMEM if x is far_ids or x is far_count else pltpu.VMEM)(x.shape, x.dtype)
             for x in operands
@@ -691,8 +740,10 @@
         + [
             pltpu.VMEM((groups, NODES, TILE, LANES), F32),
             pltpu.VMEM((vectors, points_dev), F32),
+            pltpu.VMEM((vectors, points_dev), F32),
             pltpu.SemaphoreType.DMA((len(operands),)),
             pltpu.SemaphoreType.DMA((3,)),
+            pltpu.SemaphoreType.DMA((4,)),
         ],
         compiler_params=PARAMS,
         name="down",

time: 34.4 us -> 35.1 us (1.020)
  Pallas kernels: 18.1 us -> 18.6 us
    pallas_call x1, Pallas kernels: 2.23 us -> 2.76 us  [local(): pl.pallas_call(functools.partial(middle_kernel, leaf_dev), out_shape=[sha...]
where the time goes in v2:
time: 35.1 us; the launch traced here: 34.7 us
  Pallas kernels  18.6 us (53%)
  starting transfers between devices  10.1 us (29%)
  waiting for transfers between devices  5.92 us (17%)
    pallas_call x1, Pallas kernels, local(): pl.pallas_call(side_kernel, out_shape=results, in_specs=[SMEM] + [HBM] *...  8.02 us
    all_to_all x1, starting transfers between devices, local(): lax.all_to_all(group_out, 'leaf', 0, 0, axis_index_groups=aligned, tiled=...  5.18 us
    ppermute x3, waiting for transfers between devices, shifted(): return lax.ppermute(x, 'leaf', pairs)  5.14 us
    ppermute x3, starting transfers between devices, shifted(): return lax.ppermute(x, 'leaf', pairs)  4.96 us
    pallas_call x1, Pallas kernels, local(): pl.pallas_call(functools.partial(down_kernel, len(node_parts)), out_shape...  4.84 us
    pallas_call x1, Pallas kernels, local(): pl.pallas_call(up_kernel, out_shape=[shape((GROUP, rows + edge_rows, LANE...  3.02 us
    pallas_call x1, Pallas kernels, local(): pl.pallas_call(functools.partial(middle_kernel, leaf_dev), out_shape=[sha...  2.76 us
    all_to_all x1, waiting for transfers between devices, local(): lax.all_to_all(group_out, 'leaf', 0, 0, axis_index_groups=aligned, tiled=...  0.77 us
  transfers between devices with their start and end apart: 4, of which 2 were waited for; matrix products, arithmetic and copies ran while one was open for 0% of the time, Pallas kernels for 23%

profile of v2, /device:TPU:0, one launch (start us, length us, event | category | flops | bytes accessed | tf_op | source)
XLA Modules:
  0.0 34.7 jit_solution(3301275210208142594)
XLA Ops:
  0.0 3.0 %up.1 = (f32[8,104,128]{2,1,0:T(8,128)}, f32[8,16,256]{2,1,0:T(8,128)}) custom-call(s32[1]{0:T(128)} %bitcast.me_ref, f32[16,2048]{1,0:T(8,128)} %points_hbm.1, s32[16,128]{1,0:T(8,128)} %bitcast.10, f32[8,64,256]{2,1,0:T(8,128)} %bitcast.8, f32[8,64,64]{2,1,0:T(8,128)} %refs_6_.2), custom_call_target="tpu_custom_call" | custom-call | tf_op jit(solution)/shard_map/up/pallas_call | solution.py:584
  3.0 5.2 %all-to-all-start = ((f32[8,104,128]{2,1,0:T(8,128)}), f32[8,104,128]{2,1,0:T(8,128)}, u32[]{:S(2)}, u32[]{:S(2)}) async-start(f32[8,104,128]{2,1,0:T(8,128)} %get-tuple-element.24), calls=%async_computation | async-start | bytes 851968 | tf_op jit(solution)/shard_map/all_to_all | solution.py:609
  8.2 8.0 %side.1 = (bf16[896,64]{1,0:T(8,128)(2,1)}, bf16[896,64]{1,0:T(8,128)(2,1)}, bf16[576,128]{1,0:T(8,128)(2,1)}, bf16[576,128]{1,0:T(8,128)(2,1)}, s32[16,128]{1,0...) custom-call(s32[1]{0:T(128)} %bitcast.me_ref, ...), custom_call_target="tpu_custom_call" | custom-call | flops 3000000000 | bytes 12000000 | tf_op jit(solution)/shard_map/side/pallas_call | solution.py:654
  16.2 0.8 %all-to-all-done.group_hbm.refs_3_ = f32[8,104,128]{2,1,0:T(8,128)} async-done(((f32[8,104,128]{2,1,0:T(8,128)}), f32[8,104,128]{2,1,0:T(8,128)}, u32[]{:S(2)}, u32[]{:S(2)}) %all-to-all-start) | async-done | bytes 426016 | tf_op jit(solution)/shard_map/all_to_all | solution.py:609
  17.0 2.8 %middle.1 = (f32[376,128]{1,0:T(8,128)}, f32[1,7,8,128]{3,2,1,0:T(8,128)}, f32[3,8,128]{2,1,0:T(8,128)}) custom-call(s32[1]{0:T(128)} %bitcast.me_ref, f32[8,104,128]{2,1,0:T(8,128)} %all-to-all-done.group_hbm.refs_3_, bf16[896,64]{1,0:T(8,128)(2,1)} %get-tuple-element.26.up_high_hbm, bf16[896,64]{1,0:T(8,128)(2,1)} %get-tuple-element.27.up_low_hbm), custom_call_target="tpu_custom_call" | custom-call | tf_op jit(solution)/shard_map/middle/pallas_call | solution.py:677
  19.8 1.9 %collective-permute-start.2 = (f32[376,128]{1,0:T(8,128)}, f32[376,128]{1,0:T(8,128)}, u32[]{:S(2)}, u32[]{:S(2)}) collective-permute-start(f32[376,128]{1,0:T(8,128)} %get-tuple-element.30), channel_id=1, source_target_pairs={{24,0},{25,1},{26,2},{27,3},{12,4},{13,5},{14,6},{15,7},{0,8},{1,9... | collective-permute-start | bytes 577544 | tf_op jit(solution)/shard_map/ppermute | solution.py:704
  21.7 2.1 %collective-permute-start = (f32[1,7,8,128]{3,2,1,0:T(8,128)}, f32[1,7,8,128]{3,2,1,0:T(8,128)}, u32[]{:S(2)}, u32[]{:S(2)}) collective-permute-start(f32[1,7,8,128]{3,2,1,0:T(8,128)} %get-tuple-element.28.refs_0_), channel_id=1, source_target_pairs={{8,0},{9,1},{10,2},{11,3},{28,4},{29,5},{30,6},{31,7},{16,8},{17,9... | collective-permute-start | bytes 86024 | tf_op jit(solution)/shard_map/ppermute | solution.py:704
  23.8 0.9 %collective-permute-start.1 = (f32[3,8,128]{2,1,0:T(8,128)}, f32[3,8,128]{2,1,0:T(8,128)}, u32[]{:S(2)}, u32[]{:S(2)}) collective-permute-start(f32[3,8,128]{2,1,0:T(8,128)} %get-tuple-element.29), channel_id=1, source_target_pairs={{16,0},{17,1},{18,2},{19,3},{20,4},{21,5},{22,6},{23,7},{24,8},{25... | collective-permute-start | bytes 36872 | tf_op jit(solution)/shard_map/ppermute | solution.py:704
  24.8 5.1 %collective-permute-done.1.refs_2_ = f32[3,8,128]{2,1,0:T(8,128)} collective-permute-done((f32[3,8,128]{2,1,0:T(8,128)}, f32[3,8,128]{2,1,0:T(8,128)}, u32[]{:S(2)}, u32[]{:S(2)}) %collective-permute-start.1) | collective-permute-done | bytes 12320 | tf_op jit(solution)/shard_map/ppermute | solution.py:704
  29.9 0.0 collective-permute-done.refs_1_
  29.9 0.0 collective-permute-done.2.refs_4_
  29.9 4.8 %down.1 = f32[16,2048]{1,0:T(8,128)} custom-call(s32[1]{0:T(128)} %bitcast.me_ref, f32[1,7,8,128]{3,2,1,0:T(8,128)} %get-tuple-element.28.refs_0_, f32[1,7,8,128]{3,2,1,0:T(8,128)} %collective-permute-done.refs_1_, f32[3,8,128]{2,1,0:T(8,128)} %collective-permute-done.1.refs_2_, f32[8,104,128]{2,1,0:T(8,128)} %all-to-all-done.group_hbm.refs_3_, ...), custom_call_target="tpu_custom_call" | custom-call | tf_op jit(solution)/shard_map/down/pallas_call | solution.py:731
Async XLA Ops:
  3.0 14.0 %all-to-all-start = ((f32[8,104,128]{2,1,0:T(8,128)}), f32[8,104,128]{2,1,0:T(8,128)}, u32[]{:S(2)}, u32[]{:S(2)}) async-start(f32[8,104,128]{2,1,0:T(8,128)} %get-tuple-element.24), calls=%async_computation | async-start | bytes 851968 | tf_op jit(solution)/shard_map/all_to_all | solution.py:609
  19.8 10.1 %collective-permute-start.2 = (f32[376,128]{1,0:T(8,128)}, f32[376,128]{1,0:T(8,128)}, u32[]{:S(2)}, u32[]{:S(2)}) collective-permute-start(f32[376,128]{1,0:T(8,128)} %get-tuple-element.30), channel_id=1, source_target_pairs={{24,0},{25,1},{26,2},{27,3},{12,4},{13,5},{14,6},{15,7},{0,8},{1,9... | collective-permute-start | bytes 577544 | tf_op jit(solution)/shard_map/ppermute | solution.py:704
  21.7 8.2 %collective-permute-start = (f32[1,7,8,128]{3,2,1,0:T(8,128)}, f32[1,7,8,128]{3,2,1,0:T(8,128)}, u32[]{:S(2)}, u32[]{:S(2)}) collective-permute-start(f32[1,7,8,128]{3,2,1,0:T(8,128)} %get-tuple-element.28.refs_0_), channel_id=1, source_target_pairs={{8,0},{9,1},{10,2},{11,3},{28,4},{29,5},{30,6},{31,7},{16,8},{17,9... | collective-permute-start | bytes 86024 | tf_op jit(solution)/shard_map/ppermute | solution.py:704
  23.8 6.1 %collective-permute-start.1 = (f32[3,8,128]{2,1,0:T(8,128)}, f32[3,8,128]{2,1,0:T(8,128)}, u32[]{:S(2)}, u32[]{:S(2)}) collective-permute-start(f32[3,8,128]{2,1,0:T(8,128)} %get-tuple-element.29), channel_id=1, source_target_pairs={{16,0},{17,1},{18,2},{19,3},{20,4},{21,5},{22,6},{23,7},{24,8},{25... | collective-permute-start | bytes 36872 | tf_op jit(solution)/shard_map/ppermute | solution.py:704

commit v3 on v2

--- a/solution.py
+++ b/solution.py
@@ -332,16 +332,14 @@
     group_hbm,
     up_high_hbm,
     up_low_hbm,
-    half_hbm,
+    half_out,
     nodes_out,
     far_out,
     roots_v,
     up_high,
     up_low,
-    half_out,
     sems,
     half_sems,
-    out_sems,
 ):
     low = lax.rem(me_ref[0], GROUP) < REACH
     copies = fetch(
@@ -366,10 +364,8 @@
         )
     )
     moves = fetch(moves, half_sems)
-    for copy in moves + copies:
+    for copy in copies:
         copy.wait()
-    row = REACH * rows + edge_rows
-    writes = fetch([(half_out.at[pl.ds(0, row)], half_hbm.at[pl.ds(0, row)])], out_sems)
     roots = [roots_v[peer] for peer in range(GROUP)]
     start, tiles = 0, []
     for level in range(1, DEPTH):
@@ -382,15 +378,14 @@
         nodes = dot_halves(left, up_high[start : start + size], up_low[start : start + size], NN)
         start += size
         tiles += [fold(nodes[n * 2 * TILE : (n + 1) * 2 * TILE]) for n in range(count)]
+    row = REACH * rows + edge_rows
     for index, tile in enumerate(tiles):
         half_out[row + index * TILE : row + (index + 1) * TILE, :] = tile
         for peer in range(nodes_out.shape[0]):
             nodes_out[peer, index] = tile
     for index in range(3):
         far_out[index] = tiles[NODES - 3 + index]
-    span = pl.ds(row, NODES * TILE)
-    writes += fetch([(half_out.at[span], half_hbm.at[span])], out_sems.at[pl.ds(1, 1)])
-    for copy in writes:
+    for copy in moves:
         copy.wait()
 
 
@@ -682,15 +677,13 @@
             shape((3, TILE, LANES), F32),
         ],
         in_specs=[SMEM] + [HBM] * 3,
-        out_specs=[HBM, VMEM, VMEM],
+        out_specs=[VMEM] * 3,
         scratch_shapes=[
             pltpu.VMEM((GROUP, TILE, LANES), F32),
             pltpu.VMEM(up_high.shape, BF16),
             pltpu.VMEM(up_low.shape, BF16),
-            pltpu.VMEM((REACH * rows + edge_rows + NODES * TILE, LANES), F32),
             pltpu.SemaphoreType.DMA((3,)),
             pltpu.SemaphoreType.DMA((REACH + 1,)),
-            pltpu.SemaphoreType.DMA((2,)),
         ],
         compiler_params=PARAMS,
         name="middle",

time: 35.1 us -> 34.5 us (0.983)
  Pallas kernels: 18.6 us -> 18.1 us
    pallas_call x1, Pallas kernels: 2.76 us -> 2.23 us  [local(): pl.pallas_call(functools.partial(middle_kernel, leaf_dev), out_shape=[sha...]
where the time goes in v3:
time: 34.5 us; the launch traced here: 34.2 us
  Pallas kernels  18.1 us (52%)
  starting transfers between devices  10.1 us (29%)
  waiting for transfers between devices  5.92 us (17%)
    pallas_call x1, Pallas kernels, local(): pl.pallas_call(side_kernel, out_shape=results, in_specs=[SMEM] + [HBM] *...  8.02 us
    all_to_all x1, starting transfers between devices, local(): lax.all_to_all(group_out, 'leaf', 0, 0, axis_index_groups=aligned, tiled=...  5.18 us
    ppermute x3, waiting for transfers between devices, shifted(): return lax.ppermute(x, 'leaf', pairs)  5.15 us
    ppermute x3, starting transfers between devices, shifted(): return lax.ppermute(x, 'leaf', pairs)  4.96 us
    pallas_call x1, Pallas kernels, local(): pl.pallas_call(functools.partial(down_kernel, len(node_parts)), out_shape...  4.84 us
    pallas_call x1, Pallas kernels, local(): pl.pallas_call(up_kernel, out_shape=[shape((GROUP, rows + edge_rows, LANE...  3.02 us
    pallas_call x1, Pallas kernels, local(): pl.pallas_call(functools.partial(middle_kernel, leaf_dev), out_shape=[sha...  2.23 us
    all_to_all x1, waiting for transfers between devices, local(): lax.all_to_all(group_out, 'leaf', 0, 0, axis_index_groups=aligned, tiled=...  0.77 us
  transfers between devices with their start and end apart: 4, of which 2 were waited for; matrix products, arithmetic and copies ran while one was open for 0% of the time, Pallas kernels for 23%

profile of v3, /device:TPU:0, one launch (start us, length us, event | category | flops | bytes accessed | tf_op | source)
XLA Modules:
  0.0 34.2 jit_solution(1993480115730794239)
XLA Ops:
  0.0 3.0 %up.1 = (f32[8,104,128]{2,1,0:T(8,128)}, f32[8,16,256]{2,1,0:T(8,128)}) custom-call(s32[1]{0:T(128)} %bitcast.me_ref, f32[16,2048]{1,0:T(8,128)} %points_hbm.1, s32[16,128]{1,0:T(8,128)} %bitcast.10, f32[8,64,256]{2,1,0:T(8,128)} %bitcast.8, f32[8,64,64]{2,1,0:T(8,128)} %refs_6_.2), custom_call_target="tpu_custom_call" | custom-call | tf_op jit(solution)/shard_map/up/pallas_call | solution.py:579
  3.0 5.2 %all-to-all-start = ((f32[8,104,128]{2,1,0:T(8,128)}), f32[8,104,128]{2,1,0:T(8,128)}, u32[]{:S(2)}, u32[]{:S(2)}) async-start(f32[8,104,128]{2,1,0:T(8,128)} %get-tuple-element.24), calls=%async_computation | async-start | bytes 851968 | tf_op jit(solution)/shard_map/all_to_all | solution.py:604
  8.2 8.0 %side.1 = (bf16[896,64]{1,0:T(8,128)(2,1)}, bf16[896,64]{1,0:T(8,128)(2,1)}, bf16[576,128]{1,0:T(8,128)(2,1)}, bf16[576,128]{1,0:T(8,128)(2,1)}, s32[16,128]{1,0...) custom-call(s32[1]{0:T(128)} %bitcast.me_ref, ...), custom_call_target="tpu_custom_call" | custom-call | flops 3000000000 | bytes 12000000 | tf_op jit(solution)/shard_map/side/pallas_call | solution.py:649
  16.2 0.8 %all-to-all-done.group_hbm.refs_3_ = f32[8,104,128]{2,1,0:T(8,128)} async-done(((f32[8,104,128]{2,1,0:T(8,128)}), f32[8,104,128]{2,1,0:T(8,128)}, u32[]{:S(2)}, u32[]{:S(2)}) %all-to-all-start) | async-done | bytes 426016 | tf_op jit(solution)/shard_map/all_to_all | solution.py:604
  17.0 2.2 %middle.1 = (f32[376,128]{1,0:T(8,128)}, f32[1,7,8,128]{3,2,1,0:T(8,128)}, f32[3,8,128]{2,1,0:T(8,128)}) custom-call(s32[1]{0:T(128)} %bitcast.me_ref, f32[8,104,128]{2,1,0:T(8,128)} %all-to-all-done.group_hbm.refs_3_, bf16[896,64]{1,0:T(8,128)(2,1)} %get-tuple-element.26.up_high_hbm, bf16[896,64]{1,0:T(8,128)(2,1)} %get-tuple-element.27.up_low_hbm), custom_call_target="tpu_custom_call" | custom-call | tf_op jit(solution)/shard_map/middle/pallas_call | solution.py:672
  19.3 1.9 %collective-permute-start.2 = (f32[376,128]{1,0:T(8,128)}, f32[376,128]{1,0:T(8,128)}, u32[]{:S(2)}, u32[]{:S(2)}) collective-permute-start(f32[376,128]{1,0:T(8,128)} %get-tuple-element.30), channel_id=1, source_target_pairs={{24,0},{25,1},{26,2},{27,3},{12,4},{13,5},{14,6},{15,7},{0,8},{1,9... | collective-permute-start | bytes 577544 | tf_op jit(solution)/shard_map/ppermute | solution.py:697
  21.2 2.1 %collective-permute-start = (f32[1,7,8,128]{3,2,1,0:T(8,128)}, f32[1,7,8,128]{3,2,1,0:T(8,128)}, u32[]{:S(2)}, u32[]{:S(2)}) collective-permute-start(f32[1,7,8,128]{3,2,1,0:T(8,128)} %get-tuple-element.28.refs_0_), channel_id=1, source_target_pairs={{8,0},{9,1},{10,2},{11,3},{28,4},{29,5},{30,6},{31,7},{16,8},{17,9... | collective-permute-start | bytes 86024 | tf_op jit(solution)/shard_map/ppermute | solution.py:697
  23.3 0.9 %collective-permute-start.1 = (f32[3,8,128]{2,1,0:T(8,128)}, f32[3,8,128]{2,1,0:T(8,128)}, u32[]{:S(2)}, u32[]{:S(2)}) collective-permute-start(f32[3,8,128]{2,1,0:T(8,128)} %get-tuple-element.29), channel_id=1, source_target_pairs={{16,0},{17,1},{18,2},{19,3},{20,4},{21,5},{22,6},{23,7},{24,8},{25... | collective-permute-start | bytes 36872 | tf_op jit(solution)/shard_map/ppermute | solution.py:697
  24.2 5.1 %collective-permute-done.1.refs_2_ = f32[3,8,128]{2,1,0:T(8,128)} collective-permute-done((f32[3,8,128]{2,1,0:T(8,128)}, f32[3,8,128]{2,1,0:T(8,128)}, u32[]{:S(2)}, u32[]{:S(2)}) %collective-permute-start.1) | collective-permute-done | bytes 12320 | tf_op jit(solution)/shard_map/ppermute | solution.py:697
  29.4 0.0 collective-permute-done.refs_1_
  29.4 0.0 collective-permute-done.2.refs_4_
  29.4 4.8 %down.1 = f32[16,2048]{1,0:T(8,128)} custom-call(s32[1]{0:T(128)} %bitcast.me_ref, f32[1,7,8,128]{3,2,1,0:T(8,128)} %get-tuple-element.28.refs_0_, f32[1,7,8,128]{3,2,1,0:T(8,128)} %collective-permute-done.refs_1_, f32[3,8,128]{2,1,0:T(8,128)} %collective-permute-done.1.refs_2_, f32[8,104,128]{2,1,0:T(8,128)} %all-to-all-done.group_hbm.refs_3_, ...), custom_call_target="tpu_custom_call" | custom-call | tf_op jit(solution)/shard_map/down/pallas_call | solution.py:724
Async XLA Ops:
  3.0 14.0 %all-to-all-start = ((f32[8,104,128]{2,1,0:T(8,128)}), f32[8,104,128]{2,1,0:T(8,128)}, u32[]{:S(2)}, u32[]{:S(2)}) async-start(f32[8,104,128]{2,1,0:T(8,128)} %get-tuple-element.24), calls=%async_computation | async-start | bytes 851968 | tf_op jit(solution)/shard_map/all_to_all | solution.py:604
  19.3 10.1 %collective-permute-start.2 = (f32[376,128]{1,0:T(8,128)}, f32[376,128]{1,0:T(8,128)}, u32[]{:S(2)}, u32[]{:S(2)}) collective-permute-start(f32[376,128]{1,0:T(8,128)} %get-tuple-element.30), channel_id=1, source_target_pairs={{24,0},{25,1},{26,2},{27,3},{12,4},{13,5},{14,6},{15,7},{0,8},{1,9... | collective-permute-start | bytes 577544 | tf_op jit(solution)/shard_map/ppermute | solution.py:697
  21.2 8.2 %collective-permute-start = (f32[1,7,8,128]{3,2,1,0:T(8,128)}, f32[1,7,8,128]{3,2,1,0:T(8,128)}, u32[]{:S(2)}, u32[]{:S(2)}) collective-permute-start(f32[1,7,8,128]{3,2,1,0:T(8,128)} %get-tuple-element.28.refs_0_), channel_id=1, source_target_pairs={{8,0},{9,1},{10,2},{11,3},{28,4},{29,5},{30,6},{31,7},{16,8},{17,9... | collective-permute-start | bytes 86024 | tf_op jit(solution)/shard_map/ppermute | solution.py:697
  23.3 6.1 %collective-permute-start.1 = (f32[3,8,128]{2,1,0:T(8,128)}, f32[3,8,128]{2,1,0:T(8,128)}, u32[]{:S(2)}, u32[]{:S(2)}) collective-permute-start(f32[3,8,128]{2,1,0:T(8,128)} %get-tuple-element.29), channel_id=1, source_target_pairs={{16,0},{17,1},{18,2},{19,3},{20,4},{21,5},{22,6},{23,7},{24,8},{25... | collective-permute-start | bytes 36872 | tf_op jit(solution)/shard_map/ppermute | solution.py:697

commit v4 on v0

--- a/solution.py
+++ b/solution.py
@@ -306,6 +306,7 @@
     half_out,
     nodes_out,
     far_out,
+    side_out,
     roots_v,
     up_high,
     up_low,
@@ -356,6 +357,8 @@
             nodes_out[peer, index] = tile
     for index in range(3):
         far_out[index] = tiles[NODES - 3 + index]
+        side_out[1 + index] = tiles[NODES - 3 + index]
+    side_out[0] = jnp.where(low, tiles[0], tiles[3])
     for copy in moves:
         copy.wait()
 
@@ -375,10 +378,12 @@
         near_by, far_by = jnp.where(low, groups - 1, 1), jnp.where(low, 1, groups - 1)
         across = lax.rem(group + 2, groups)
         near_group = lax.rem(group + near_by, groups)
+        far_group = lax.rem(group + far_by, groups)
         node_copies = fetch(
             [
                 (node_parts[0].at[0], nodes_ref.at[group]),
-                (node_parts[1].at[0], nodes_ref.at[lax.rem(group + far_by, groups)]),
+                (node_parts[1].at[0], nodes_ref.at[far_group, jnp.where(low, 0, 3)]),
+                (node_parts[1].at[pl.ds(1, 3)], nodes_ref.at[far_group, pl.ds(NODES - 3, 3)]),
                 (node_parts[2], nodes_ref.at[across, pl.ds(NODES - 3, 3)]),
             ],
             node_sems,
@@ -627,15 +632,16 @@
     )(me, *operands)
 
     by_permute = groups == 4
-    half_out, nodes_out, far_nodes = pl.pallas_call(
+    half_out, nodes_out, far_nodes, side_nodes = pl.pallas_call(
         functools.partial(middle_kernel, leaf_dev),
         out_shape=[
             shape((REACH * rows + edge_rows + NODES * TILE, LANES), F32),
             shape((1 if by_permute else groups, NODES, TILE, LANES), F32),
             shape((3, TILE, LANES), F32),
+            shape((4, TILE, LANES), F32),
         ],
         in_specs=[SMEM] + [HBM] * 3,
-        out_specs=[VMEM] * 3,
+        out_specs=[VMEM] * 4,
         scratch_shapes=[
             pltpu.VMEM((GROUP, TILE, LANES), F32),
             pltpu.VMEM(up_high.shape, BF16),
@@ -656,7 +662,7 @@
 
     half_in = shifted(half_out, -1, 1)
     if by_permute:
-        node_parts = (nodes_out, shifted(nodes_out, 1, -1), shifted(far_nodes, 2, 2))
+        node_parts = (nodes_out, shifted(side_nodes, 1, -1), shifted(far_nodes, 2, 2))
     else:
         across = [[g * GROUP + i for g in range(groups)] for i in range(GROUP)]
         node_parts = (lax.all_to_all(nodes_out, "leaf", 0, 0, axis_index_groups=across, tiled=True),)
@@ -692,7 +698,7 @@
             pltpu.VMEM((groups, NODES, TILE, LANES), F32),
             pltpu.VMEM((vectors, points_dev), F32),
             pltpu.SemaphoreType.DMA((len(operands),)),
-            pltpu.SemaphoreType.DMA((3,)),
+            pltpu.SemaphoreType.DMA((4,)),
         ],
         compiler_params=PARAMS,
         name="down",

time: 34.4 us -> 34.1 us (level)
  transfers between devices with their start and end apart: 4 -> 4, of which waited for: 2 -> 2; matrix products, arithmetic and copies ran while one was open for 0% -> 0% of each run, Pallas kernels for 23% -> 24%
where the time goes in v4:
time: 34.1 us; the launch traced here: 33.9 us
  Pallas kernels  18.1 us (53%)
  starting transfers between devices  10.1 us (30%)
  waiting for transfers between devices  5.66 us (17%)
    pallas_call x1, Pallas kernels, local(): pl.pallas_call(side_kernel, out_shape=results, in_specs=[SMEM] + [HBM] *...  8.02 us
    all_to_all x1, starting transfers between devices, local(): lax.all_to_all(group_out, 'leaf', 0, 0, axis_index_groups=aligned, tiled=...  5.19 us
    ppermute x3, starting transfers between devices, shifted(): return lax.ppermute(x, 'leaf', pairs)  4.96 us
    ppermute x3, waiting for transfers between devices, shifted(): return lax.ppermute(x, 'leaf', pairs)  4.88 us
    pallas_call x1, Pallas kernels, local(): pl.pallas_call(functools.partial(down_kernel, len(node_parts)), out_shape...  4.82 us
    pallas_call x1, Pallas kernels, local(): pl.pallas_call(up_kernel, out_shape=[shape((GROUP, rows + edge_rows, LANE...  2.99 us
    pallas_call x1, Pallas kernels, local(): pl.pallas_call(functools.partial(middle_kernel, leaf_dev), out_shape=[sha...  2.24 us
    all_to_all x1, waiting for transfers between devices, local(): lax.all_to_all(group_out, 'leaf', 0, 0, axis_index_groups=aligned, tiled=...  0.77 us
  transfers between devices with their start and end apart: 4, of which 2 were waited for; matrix products, arithmetic and copies ran while one was open for 0% of the time, Pallas kernels for 24%

profile of v4, /device:TPU:0, one launch (start us, length us, event | category | flops | bytes accessed | tf_op | source)
XLA Modules:
  0.0 33.9 jit_solution(9864065259880973428)
XLA Ops:
  0.0 3.0 %up.1 = (f32[8,104,128]{2,1,0:T(8,128)}, f32[8,16,256]{2,1,0:T(8,128)}) custom-call(s32[1]{0:T(128)} %bitcast.me_ref, f32[16,2048]{1,0:T(8,128)} %points_hbm.1, s32[16,128]{1,0:T(8,128)} %bitcast.10, f32[8,64,256]{2,1,0:T(8,128)} %bitcast.8, f32[8,64,64]{2,1,0:T(8,128)} %refs_6_.2), custom_call_target="tpu_custom_call" | custom-call | tf_op jit(solution)/shard_map/up/pallas_call | solution.py:547
  3.0 5.2 %all-to-all-start = ((f32[8,104,128]{2,1,0:T(8,128)}), f32[8,104,128]{2,1,0:T(8,128)}, u32[]{:S(2)}, u32[]{:S(2)}) async-start(f32[8,104,128]{2,1,0:T(8,128)} %get-tuple-element.25), calls=%async_computation | async-start | bytes 851968 | tf_op jit(solution)/shard_map/all_to_all | solution.py:567
  8.2 8.0 %side.1 = (bf16[896,64]{1,0:T(8,128)(2,1)}, bf16[896,64]{1,0:T(8,128)(2,1)}, bf16[576,128]{1,0:T(8,128)(2,1)}, bf16[576,128]{1,0:T(8,128)(2,1)}, s32[16,128]{1,0...) custom-call(s32[1]{0:T(128)} %bitcast.me_ref, ...), custom_call_target="tpu_custom_call" | custom-call | flops 3000000000 | bytes 12000000 | tf_op jit(solution)/shard_map/side/pallas_call | solution.py:612
  16.2 0.8 %all-to-all-done.group_hbm.refs_3_ = f32[8,104,128]{2,1,0:T(8,128)} async-done(((f32[8,104,128]{2,1,0:T(8,128)}), f32[8,104,128]{2,1,0:T(8,128)}, u32[]{:S(2)}, u32[]{:S(2)}) %all-to-all-start) | async-done | bytes 426016 | tf_op jit(solution)/shard_map/all_to_all | solution.py:567
  17.0 2.2 %middle.1 = (f32[376,128]{1,0:T(8,128)}, f32[1,7,8,128]{3,2,1,0:T(8,128)}, f32[3,8,128]{2,1,0:T(8,128)}, f32[4,8,128]{2,1,0:T(8,128)}) custom-call(s32[1]{0:T(128)} %bitcast.me_ref, f32[8,104,128]{2,1,0:T(8,128)} %all-to-all-done.group_hbm.refs_3_, bf16[896,64]{1,0:T(8,128)(2,1)} %get-tuple-element.27.up_high_hbm, bf16[896,64]{1,0:T(8,128)(2,1)} %get-tuple-element.28.up_low_hbm), custom_call_target="tpu_custom_call" | custom-call | tf_op jit(solution)/shard_map/middle/pallas_call | solution.py:635
  19.2 1.9 %collective-permute-start.2 = (f32[376,128]{1,0:T(8,128)}, f32[376,128]{1,0:T(8,128)}, u32[]{:S(2)}, u32[]{:S(2)}) collective-permute-start(f32[376,128]{1,0:T(8,128)} %get-tuple-element.32), channel_id=1, source_target_pairs={{24,0},{25,1},{26,2},{27,3},{12,4},{13,5},{14,6},{15,7},{0,8},{1,9... | collective-permute-start | bytes 577544 | tf_op jit(solution)/shard_map/ppermute | solution.py:661
  21.2 2.1 %collective-permute-start = (f32[4,8,128]{2,1,0:T(8,128)}, f32[4,8,128]{2,1,0:T(8,128)}, u32[]{:S(2)}, u32[]{:S(2)}) collective-permute-start(f32[4,8,128]{2,1,0:T(8,128)} %get-tuple-element.30), channel_id=1, source_target_pairs={{8,0},{9,1},{10,2},{11,3},{28,4},{29,5},{30,6},{31,7},{16,8},{17,9... | collective-permute-start | bytes 49160 | tf_op jit(solution)/shard_map/ppermute | solution.py:661
  23.2 0.9 %collective-permute-start.1 = (f32[3,8,128]{2,1,0:T(8,128)}, f32[3,8,128]{2,1,0:T(8,128)}, u32[]{:S(2)}, u32[]{:S(2)}) collective-permute-start(f32[3,8,128]{2,1,0:T(8,128)} %get-tuple-element.31), channel_id=1, source_target_pairs={{16,0},{17,1},{18,2},{19,3},{20,4},{21,5},{22,6},{23,7},{24,8},{25... | collective-permute-start | bytes 36872 | tf_op jit(solution)/shard_map/ppermute | solution.py:661
  24.2 4.9 %collective-permute-done.1.refs_2_ = f32[3,8,128]{2,1,0:T(8,128)} collective-permute-done((f32[3,8,128]{2,1,0:T(8,128)}, f32[3,8,128]{2,1,0:T(8,128)}, u32[]{:S(2)}, u32[]{:S(2)}) %collective-permute-start.1) | collective-permute-done | bytes 12320 | tf_op jit(solution)/shard_map/ppermute | solution.py:661
  29.1 0.0 collective-permute-done.refs_1_
  29.1 0.0 collective-permute-done.2.refs_4_
  29.1 4.8 %down.1 = f32[16,2048]{1,0:T(8,128)} custom-call(s32[1]{0:T(128)} %bitcast.me_ref, f32[1,7,8,128]{3,2,1,0:T(8,128)} %get-tuple-element.29.refs_0_, f32[4,8,128]{2,1,0:T(8,128)} %collective-permute-done.refs_1_, f32[3,8,128]{2,1,0:T(8,128)} %collective-permute-done.1.refs_2_, f32[8,104,128]{2,1,0:T(8,128)} %all-to-all-done.group_hbm.refs_3_, ...), custom_call_target="tpu_custom_call" | custom-call | tf_op jit(solution)/shard_map/down/pallas_call | solution.py:688
Async XLA Ops:
  3.0 14.0 %all-to-all-start = ((f32[8,104,128]{2,1,0:T(8,128)}), f32[8,104,128]{2,1,0:T(8,128)}, u32[]{:S(2)}, u32[]{:S(2)}) async-start(f32[8,104,128]{2,1,0:T(8,128)} %get-tuple-element.25), calls=%async_computation | async-start | bytes 851968 | tf_op jit(solution)/shard_map/all_to_all | solution.py:567
  19.2 9.8 %collective-permute-start.2 = (f32[376,128]{1,0:T(8,128)}, f32[376,128]{1,0:T(8,128)}, u32[]{:S(2)}, u32[]{:S(2)}) collective-permute-start(f32[376,128]{1,0:T(8,128)} %get-tuple-element.32), channel_id=1, source_target_pairs={{24,0},{25,1},{26,2},{27,3},{12,4},{13,5},{14,6},{15,7},{0,8},{1,9... | collective-permute-start | bytes 577544 | tf_op jit(solution)/shard_map/ppermute | solution.py:661
  21.2 7.9 %collective-permute-start = (f32[4,8,128]{2,1,0:T(8,128)}, f32[4,8,128]{2,1,0:T(8,128)}, u32[]{:S(2)}, u32[]{:S(2)}) collective-permute-start(f32[4,8,128]{2,1,0:T(8,128)} %get-tuple-element.30), channel_id=1, source_target_pairs={{8,0},{9,1},{10,2},{11,3},{28,4},{29,5},{30,6},{31,7},{16,8},{17,9... | collective-permute-start | bytes 49160 | tf_op jit(solution)/shard_map/ppermute | solution.py:661
  23.2 5.8 %collective-permute-start.1 = (f32[3,8,128]{2,1,0:T(8,128)}, f32[3,8,128]{2,1,0:T(8,128)}, u32[]{:S(2)}, u32[]{:S(2)}) collective-permute-start(f32[3,8,128]{2,1,0:T(8,128)} %get-tuple-element.31), channel_id=1, source_target_pairs={{16,0},{17,1},{18,2},{19,3},{20,4},{21,5},{22,6},{23,7},{24,8},{25... | collective-permute-start | bytes 36872 | tf_op jit(solution)/shard_map/ppermute | solution.py:661

commit v5 on v4

--- a/solution.py
+++ b/solution.py
@@ -356,9 +356,10 @@
         for peer in range(nodes_out.shape[0]):
             nodes_out[peer, index] = tile
     for index in range(3):
-        far_out[index] = tiles[NODES - 3 + index]
         side_out[1 + index] = tiles[NODES - 3 + index]
     side_out[0] = jnp.where(low, tiles[0], tiles[3])
+    far_out[0] = jnp.where(low, tiles[5], tiles[4])
+    far_out[1] = tiles[6]
     for copy in moves:
         copy.wait()
 
@@ -384,7 +385,8 @@
                 (node_parts[0].at[0], nodes_ref.at[group]),
                 (node_parts[1].at[0], nodes_ref.at[far_group, jnp.where(low, 0, 3)]),
                 (node_parts[1].at[pl.ds(1, 3)], nodes_ref.at[far_group, pl.ds(NODES - 3, 3)]),
-                (node_parts[2], nodes_ref.at[across, pl.ds(NODES - 3, 3)]),
+                (node_parts[2].at[0], nodes_ref.at[across, jnp.where(low, 5, 4)]),
+                (node_parts[2].at[1], nodes_ref.at[across, NODES - 1]),
             ],
             node_sems,
         )
@@ -637,7 +639,7 @@
         out_shape=[
             shape((REACH * rows + edge_rows + NODES * TILE, LANES), F32),
             shape((1 if by_permute else groups, NODES, TILE, LANES), F32),
-            shape((3, TILE, LANES), F32),
+            shape((2, TILE, LANES), F32),
             shape((4, TILE, LANES), F32),
         ],
         in_specs=[SMEM] + [HBM] * 3,
@@ -698,7 +700,7 @@
             pltpu.VMEM((groups, NODES, TILE, LANES), F32),
             pltpu.VMEM((vectors, points_dev), F32),
             pltpu.SemaphoreType.DMA((len(operands),)),
-            pltpu.SemaphoreType.DMA((4,)),
+            pltpu.SemaphoreType.DMA((5,)),
         ],
         compiler_params=PARAMS,
         name="down",

time: 34.1 us -> 33.9 us (level)
  no operation moved by 1% of the time
where the time goes in v5:
time: 33.9 us; the launch traced here: 33.7 us
  Pallas kernels  18 us (53%)
  starting transfers between devices  10.1 us (30%)
  waiting for transfers between devices  5.48 us (16%)
    pallas_call x1, Pallas kernels, local(): pl.pallas_call(side_kernel, out_shape=results, in_specs=[SMEM] + [HBM] *...  8.02 us
    all_to_all x1, starting transfers between devices, local(): lax.all_to_all(group_out, 'leaf', 0, 0, axis_index_groups=aligned, tiled=...  5.19 us
    ppermute x3, starting transfers between devices, shifted(): return lax.ppermute(x, 'leaf', pairs)  4.96 us
    pallas_call x1, Pallas kernels, local(): pl.pallas_call(functools.partial(down_kernel, len(node_parts)), out_shape...  4.79 us
    ppermute x3, waiting for transfers between devices, shifted(): return lax.ppermute(x, 'leaf', pairs)  4.71 us
    pallas_call x1, Pallas kernels, local(): pl.pallas_call(up_kernel, out_shape=[shape((GROUP, rows + edge_rows, LANE...  2.99 us
    pallas_call x1, Pallas kernels, local(): pl.pallas_call(functools.partial(middle_kernel, leaf_dev), out_shape=[sha...  2.24 us
    all_to_all x1, waiting for transfers between devices, local(): lax.all_to_all(group_out, 'leaf', 0, 0, axis_index_groups=aligned, tiled=...  0.77 us
  transfers between devices with their start and end apart: 4, of which 2 were waited for; matrix products, arithmetic and copies ran while one was open for 0% of the time, Pallas kernels for 24%

profile of v5, /device:TPU:0, one launch (start us, length us, event | category | flops | bytes accessed | tf_op | source)
XLA Modules:
  0.0 33.7 jit_solution(4793618702333041077)
XLA Ops:
  0.0 3.0 %up.1 = (f32[8,104,128]{2,1,0:T(8,128)}, f32[8,16,256]{2,1,0:T(8,128)}) custom-call(s32[1]{0:T(128)} %bitcast.me_ref, f32[16,2048]{1,0:T(8,128)} %points_hbm.1, s32[16,128]{1,0:T(8,128)} %bitcast.10, f32[8,64,256]{2,1,0:T(8,128)} %bitcast.8, f32[8,64,64]{2,1,0:T(8,128)} %refs_6_.2), custom_call_target="tpu_custom_call" | custom-call | tf_op jit(solution)/shard_map/up/pallas_call | solution.py:549
  3.0 5.2 %all-to-all-start = ((f32[8,104,128]{2,1,0:T(8,128)}), f32[8,104,128]{2,1,0:T(8,128)}, u32[]{:S(2)}, u32[]{:S(2)}) async-start(f32[8,104,128]{2,1,0:T(8,128)} %get-tuple-element.25), calls=%async_computation | async-start | bytes 851968 | tf_op jit(solution)/shard_map/all_to_all | solution.py:569
  8.2 8.0 %side.1 = (bf16[896,64]{1,0:T(8,128)(2,1)}, bf16[896,64]{1,0:T(8,128)(2,1)}, bf16[576,128]{1,0:T(8,128)(2,1)}, bf16[576,128]{1,0:T(8,128)(2,1)}, s32[16,128]{1,0...) custom-call(s32[1]{0:T(128)} %bitcast.me_ref, ...), custom_call_target="tpu_custom_call" | custom-call | flops 3000000000 | bytes 12000000 | tf_op jit(solution)/shard_map/side/pallas_call | solution.py:614
  16.2 0.8 %all-to-all-done.group_hbm.refs_3_ = f32[8,104,128]{2,1,0:T(8,128)} async-done(((f32[8,104,128]{2,1,0:T(8,128)}), f32[8,104,128]{2,1,0:T(8,128)}, u32[]{:S(2)}, u32[]{:S(2)}) %all-to-all-start) | async-done | bytes 426016 | tf_op jit(solution)/shard_map/all_to_all | solution.py:569
  17.0 2.2 %middle.1 = (f32[376,128]{1,0:T(8,128)}, f32[1,7,8,128]{3,2,1,0:T(8,128)}, f32[2,8,128]{2,1,0:T(8,128)}, f32[4,8,128]{2,1,0:T(8,128)}) custom-call(s32[1]{0:T(128)} %bitcast.me_ref, f32[8,104,128]{2,1,0:T(8,128)} %all-to-all-done.group_hbm.refs_3_, bf16[896,64]{1,0:T(8,128)(2,1)} %get-tuple-element.27.up_high_hbm, bf16[896,64]{1,0:T(8,128)(2,1)} %get-tuple-element.28.up_low_hbm), custom_call_target="tpu_custom_call" | custom-call | tf_op jit(solution)/shard_map/middle/pallas_call | solution.py:637
  19.2 1.9 %collective-permute-start.2 = (f32[376,128]{1,0:T(8,128)}, f32[376,128]{1,0:T(8,128)}, u32[]{:S(2)}, u32[]{:S(2)}) collective-permute-start(f32[376,128]{1,0:T(8,128)} %get-tuple-element.32), channel_id=1, source_target_pairs={{24,0},{25,1},{26,2},{27,3},{12,4},{13,5},{14,6},{15,7},{0,8},{1,9... | collective-permute-start | bytes 577544 | tf_op jit(solution)/shard_map/ppermute | solution.py:663
  21.2 2.1 %collective-permute-start = (f32[4,8,128]{2,1,0:T(8,128)}, f32[4,8,128]{2,1,0:T(8,128)}, u32[]{:S(2)}, u32[]{:S(2)}) collective-permute-start(f32[4,8,128]{2,1,0:T(8,128)} %get-tuple-element.30), channel_id=1, source_target_pairs={{8,0},{9,1},{10,2},{11,3},{28,4},{29,5},{30,6},{31,7},{16,8},{17,9... | collective-permute-start | bytes 49160 | tf_op jit(solution)/shard_map/ppermute | solution.py:663
  23.2 0.9 %collective-permute-start.1 = (f32[2,8,128]{2,1,0:T(8,128)}, f32[2,8,128]{2,1,0:T(8,128)}, u32[]{:S(2)}, u32[]{:S(2)}) collective-permute-start(f32[2,8,128]{2,1,0:T(8,128)} %get-tuple-element.31), channel_id=1, source_target_pairs={{16,0},{17,1},{18,2},{19,3},{20,4},{21,5},{22,6},{23,7},{24,8},{25... | collective-permute-start | bytes 24584 | tf_op jit(solution)/shard_map/ppermute | solution.py:663
  24.2 4.7 %collective-permute-done.1.refs_2_ = f32[2,8,128]{2,1,0:T(8,128)} collective-permute-done((f32[2,8,128]{2,1,0:T(8,128)}, f32[2,8,128]{2,1,0:T(8,128)}, u32[]{:S(2)}, u32[]{:S(2)}) %collective-permute-start.1) | collective-permute-done | bytes 8224 | tf_op jit(solution)/shard_map/ppermute | solution.py:663
  28.9 0.0 collective-permute-done.refs_1_
  28.9 0.0 collective-permute-done.2.refs_4_
  28.9 4.8 %down.1 = f32[16,2048]{1,0:T(8,128)} custom-call(s32[1]{0:T(128)} %bitcast.me_ref, f32[1,7,8,128]{3,2,1,0:T(8,128)} %get-tuple-element.29.refs_0_, f32[4,8,128]{2,1,0:T(8,128)} %collective-permute-done.refs_1_, f32[2,8,128]{2,1,0:T(8,128)} %collective-permute-done.1.refs_2_, f32[8,104,128]{2,1,0:T(8,128)} %all-to-all-done.group_hbm.refs_3_, ...), custom_call_target="tpu_custom_call" | custom-call | tf_op jit(solution)/shard_map/down/pallas_call | solution.py:690
Async XLA Ops:
  3.0 14.0 %all-to-all-start = ((f32[8,104,128]{2,1,0:T(8,128)}), f32[8,104,128]{2,1,0:T(8,128)}, u32[]{:S(2)}, u32[]{:S(2)}) async-start(f32[8,104,128]{2,1,0:T(8,128)} %get-tuple-element.25), calls=%async_computation | async-start | bytes 851968 | tf_op jit(solution)/shard_map/all_to_all | solution.py:569
  19.2 9.7 %collective-permute-start.2 = (f32[376,128]{1,0:T(8,128)}, f32[376,128]{1,0:T(8,128)}, u32[]{:S(2)}, u32[]{:S(2)}) collective-permute-start(f32[376,128]{1,0:T(8,128)} %get-tuple-element.32), channel_id=1, source_target_pairs={{24,0},{25,1},{26,2},{27,3},{12,4},{13,5},{14,6},{15,7},{0,8},{1,9... | collective-permute-start | bytes 577544 | tf_op jit(solution)/shard_map/ppermute | solution.py:663
  21.2 7.7 %collective-permute-start = (f32[4,8,128]{2,1,0:T(8,128)}, f32[4,8,128]{2,1,0:T(8,128)}, u32[]{:S(2)}, u32[]{:S(2)}) collective-permute-start(f32[4,8,128]{2,1,0:T(8,128)} %get-tuple-element.30), channel_id=1, source_target_pairs={{8,0},{9,1},{10,2},{11,3},{28,4},{29,5},{30,6},{31,7},{16,8},{17,9... | collective-permute-start | bytes 49160 | tf_op jit(solution)/shard_map/ppermute | solution.py:663
  23.2 5.6 %collective-permute-start.1 = (f32[2,8,128]{2,1,0:T(8,128)}, f32[2,8,128]{2,1,0:T(8,128)}, u32[]{:S(2)}, u32[]{:S(2)}) collective-permute-start(f32[2,8,128]{2,1,0:T(8,128)} %get-tuple-element.31), channel_id=1, source_target_pairs={{16,0},{17,1},{18,2},{19,3},{20,4},{21,5},{22,6},{23,7},{24,8},{25... | collective-permute-start | bytes 24584 | tf_op jit(solution)/shard_map/ppermute | solution.py:663
